TPU v7x, 32 devices: a whole 2x2x4 slice. The times are simulated.
32 devices in a mesh: dp: 8 (over z, y), head: 4 (over x, core).
Axes of the slice: x: 2, y: 2, z: 4, core: 2. Of those that a mesh axis runs over, the one named last changes fastest.
Arguments:
- latents: bfloat16 [64, 128, 768], P('dp'), may hold values from -6 to 6
- byte_array: bfloat16 [64, 616, 768], P('dp'), may hold values from -6 to 6
- cotangent: bfloat16 [64, 128, 768], P('dp'), may hold values from -6 to 6
- patch_count: int32 [64], P('dp'), may hold values from 196 to 576, as said below
- text_len: int32 [64], P('dp'), may hold values from 1 to 40, as said below
- inner_weight: float32 [3, 768, 768], P(None, 'dp', 'head'), may hold values from -0.21875 to 0.21875
- inner_moment: float32 [3, 768, 768], P(None, 'dp', 'head'), may hold values from -0.0625 to 0.0625
- inner_square: float32 [3, 768, 768], P(None, 'dp', 'head'), may hold values from 0.0001 to 0.0004
- output_weight: float32 [768, 768], P('head', 'dp')
- output_moment: float32 [768, 768], P('head', 'dp'), may hold values from -0.0625 to 0.0625
- output_square: float32 [768, 768], P('head', 'dp'), may hold values from 0.0001 to 0.0004
- expand_weight: float32 [768, 3072], P('dp', 'head'), may hold values from -0.21875 to 0.21875
- expand_moment: float32 [768, 3072], P('dp', 'head'), may hold values from -0.0625 to 0.0625
- expand_square: float32 [768, 3072], P('dp', 'head'), may hold values from 0.0001 to 0.0004
- reduce_weight: float32 [3072, 768], P('head', 'dp')
- reduce_moment: float32 [3072, 768], P('head', 'dp'), may hold values from -0.0625 to 0.0625
- reduce_square: float32 [3072, 768], P('head', 'dp'), may hold values from 0.0001 to 0.0004
- expand_bias: float32 [3072], P('head'), may hold values from -3 to 3
- bias_moment: float32 [3072], P('head'), may hold values from -0.0625 to 0.0625
- bias_square: float32 [3072], P('head'), may hold values from 0.0001 to 0.0004
- norm_vectors: float32 [7, 768], replicated
- vector_moment: float32 [7, 768], replicated, may hold values from -0.1875 to 0.1875
- vector_square: float32 [7, 768], replicated, may hold values from 0.0009 to 0.0036
Outputs:
- block_output: bfloat16 [64, 128, 768], P('dp')
- latent_gradient: bfloat16 [64, 128, 768], P('dp')
- byte_gradient: bfloat16 [64, 616, 768], P('dp', 'head')
- inner_updated: float32 [3, 768, 768], P(None, 'dp', 'head')
- inner_moment_new: float32 [3, 768, 768], P(None, 'dp', 'head')
- inner_square_new: float32 [3, 768, 768], P(None, 'dp', 'head')
- output_updated: float32 [768, 768], P('head', 'dp')
- output_moment_new: float32 [768, 768], P('head', 'dp')
- output_square_new: float32 [768, 768], P('head', 'dp')
- expand_updated: float32 [768, 3072], P('dp', 'head')
- expand_moment_new: float32 [768, 3072], P('dp', 'head')
- expand_square_new: float32 [768, 3072], P('dp', 'head')
- reduce_updated: float32 [3072, 768], P('head', 'dp')
- reduce_moment_new: float32 [3072, 768], P('head', 'dp')
- reduce_square_new: float32 [3072, 768], P('head', 'dp')
- bias_updated: float32 [3072], P('head')
- bias_moment_new: float32 [3072], P('head')
- bias_square_new: float32 [3072], P('head')
- vector_updated: float32 [7, 768], replicated
- vector_moment_new: float32 [7, 768], replicated
- vector_square_new: float32 [7, 768], replicated
- grad_norm: float32 [], replicated
Inputs may be any that keep to these rules, and one draw needn't show every extreme that they name: `patch_count`: each item's count is 196 or 576; both occur in every draw. `text_len`: some item has 40.
All inputs are finite; a program needn't handle non-finite values.
Results may differ from a plain program's by a relative error of at most 0.013.
The roundings to bfloat16 on the way count: a program that leaves them out, or rounds other values in their place, can miss the bound.
Values may be sent and summed in bfloat16 or wider, within the bound.
No kernel may reach another device: no remote copies, remote signals or barrier semaphores. Data moves between devices by JAX's collectives and lax.ppermute only.
A program may use at most 192 MiB of HBM per device.

v0:
```python
import math

import jax
import jax.numpy as jnp
from jax import lax
from jax.sharding import PartitionSpec as P

D = 768
HEAD_DIM = 64
FF = 3072
PATCHES = 576
FRAMES = 1
STEP = 5


NEG_FILL = -1000000000.0
BETA = 0.5
ADAM_EPS = 1e-08
DECAY = 0.01
CLIP_RATE = 0.01


def layer_norm(inputs, gain_row, bias_row):
    centred = inputs - jnp.mean(inputs, -1, keepdims=True)
    variance = jnp.mean(centred * centred, -1, keepdims=True)
    return centred * lax.rsqrt(variance + 1e-05) * gain_row + bias_row


def exact_gelu(values):
    return jax.nn.gelu(values, approximate=False)


def key_valid(patch_count, text_len, keys_total):
    slot = jnp.arange(keys_total, dtype=jnp.int32)
    patch_slot = (slot[None, :] < FRAMES * PATCHES) & (
        slot[None, :] % PATCHES < patch_count[:, None]
    )
    text_slot = (slot[None, :] >= FRAMES * PATCHES) & (
        slot[None, :] - FRAMES * PATCHES < text_len[:, None]
    )
    return patch_slot | text_slot


def adamw(weight, moment, square, gradient, rate, decay_rate):
    moment_new = BETA * moment + (1.0 - BETA) * gradient
    square_new = BETA * square + (1.0 - BETA) * gradient * gradient
    correction = 1.0 - BETA**STEP
    step_dir = moment_new / correction / (jnp.sqrt(square_new / correction) + ADAM_EPS)
    return (weight - rate * (step_dir + decay_rate * weight), moment_new, square_new)


def head_total(partial_value):
    return lax.psum(partial_value, "head")


def body(
    latents,
    byte_array,
    cotangent,
    patch_count,
    text_len,
    inner_weight,
    inner_moment,
    inner_square,
    output_weight,
    output_moment,
    output_square,
    expand_weight,
    expand_moment,
    expand_square,
    reduce_weight,
    reduce_moment,
    reduce_square,
    expand_bias,
    bias_moment,
    bias_square,
    norm_vectors,
    vector_moment,
    vector_square,
):
    item_count, lat_len, width = latents.shape
    keys_total = byte_array.shape[1]
    head_count = lax.axis_size("head")
    head_index = lax.axis_index("head")
    local_width = inner_weight.shape[2]
    local_heads = local_width // HEAD_DIM
    scale = 1.0 / math.sqrt(HEAD_DIM)
    first_head = (head_index == 0).astype(jnp.float32)
    inner_full, output_full, expand_full, reduce_full = (
        lax.all_gather(inner_weight.astype(jnp.bfloat16), "dp", axis=1, tiled=True),
        lax.all_gather(output_weight.astype(jnp.bfloat16), "dp", axis=1, tiled=True),
        lax.all_gather(expand_weight.astype(jnp.bfloat16), "dp", axis=0, tiled=True),
        lax.all_gather(reduce_weight.astype(jnp.bfloat16), "dp", axis=1, tiled=True),
    )
    query_w = inner_full[0]
    key_value_w = jnp.concatenate([inner_full[1], inner_full[2]], axis=1)
    lat_float = latents.astype(jnp.float32)
    byte_float = byte_array.astype(jnp.float32)
    upstream = cotangent.astype(jnp.float32)
    latent_norm = layer_norm(lat_float, norm_vectors[0], norm_vectors[1]).astype(jnp.bfloat16)
    byte_norm = layer_norm(byte_float, norm_vectors[2], norm_vectors[3]).astype(jnp.bfloat16)
    queries = jnp.einsum(
        "ild,de->ile", latent_norm, query_w, preferred_element_type=jnp.float32
    ).astype(jnp.bfloat16)
    key_value = jnp.einsum(
        "ikd,de->ike", byte_norm, key_value_w, preferred_element_type=jnp.float32
    ).astype(jnp.bfloat16)
    query_heads = queries.reshape(item_count, lat_len, local_heads, HEAD_DIM)
    key_heads = key_value[:, :, :local_width].reshape(item_count, keys_total, local_heads, HEAD_DIM)
    value_heads = key_value[:, :, local_width:].reshape(
        item_count, keys_total, local_heads, HEAD_DIM
    )
    valid = key_valid(patch_count, text_len, keys_total)[:, None, None, :]

    def masked_scores():
        raw_scores = (
            jnp.einsum(
                "ilhe,ikhe->ihlk", query_heads, key_heads, preferred_element_type=jnp.float32
            )
            * scale
        )
        return jnp.where(valid, raw_scores, NEG_FILL)

    masked = masked_scores()
    row_top = jnp.max(masked, -1, keepdims=True)
    expo = jnp.exp(masked - row_top)
    row_total = jnp.sum(expo, -1, keepdims=True)
    log_total = row_top + jnp.log(row_total)
    attention = (expo / row_total).astype(jnp.bfloat16)
    mixed = jnp.einsum(
        "ihlk,ikhe->ilhe", attention, value_heads, preferred_element_type=jnp.float32
    )
    mixed = mixed.astype(jnp.bfloat16).reshape(item_count, lat_len, local_width)
    attn_part = jnp.einsum("ile,ed->ild", mixed, output_full, preferred_element_type=jnp.float32)
    residual = lat_float + head_total(attn_part)
    mlp_norm = layer_norm(residual, norm_vectors[4], norm_vectors[5]).astype(jnp.bfloat16)
    pre_act = (
        jnp.einsum("ild,df->ilf", mlp_norm, expand_full, preferred_element_type=jnp.float32)
        + expand_bias
    )
    hidden = exact_gelu(pre_act).astype(jnp.bfloat16)
    mlp_part = jnp.einsum("ilf,fd->ild", hidden, reduce_full, preferred_element_type=jnp.float32)
    block_output = (residual + head_total(mlp_part) + norm_vectors[6]).astype(jnp.bfloat16)
    bias_out_grad = jnp.sum(upstream, (0, 1))
    reduce_grad = jnp.einsum("ilf,ild->fd", hidden, cotangent, preferred_element_type=jnp.float32)
    hidden_grad = jnp.einsum(
        "ild,fd->ilf", cotangent, reduce_full, preferred_element_type=jnp.float32
    )
    gelu_pull = jax.vjp(exact_gelu, pre_act)[1]
    pre_grad = gelu_pull(hidden_grad)[0].astype(jnp.bfloat16)
    expand_bias_grad = jnp.sum(pre_grad.astype(jnp.float32), (0, 1))
    expand_grad = jnp.einsum("ild,ilf->df", mlp_norm, pre_grad, preferred_element_type=jnp.float32)
    mlp_norm_part = jnp.einsum(
        "ilf,df->ild", pre_grad, expand_full, preferred_element_type=jnp.float32
    )
    mlp_norm_grad = head_total(mlp_norm_part)
    mlp_pull = jax.vjp(layer_norm, residual, norm_vectors[4], norm_vectors[5])[1]
    norm_res_grad, gain_mlp_grad, bias_mlp_grad = mlp_pull(mlp_norm_grad)
    residual_grad = upstream + norm_res_grad
    residual_low = residual_grad.astype(jnp.bfloat16)
    output_grad = jnp.einsum("ile,ild->ed", mixed, residual_low, preferred_element_type=jnp.float32)
    mixed_grad = jnp.einsum(
        "ild,ed->ile", residual_low, output_full, preferred_element_type=jnp.float32
    )
    mixed_grad = mixed_grad.astype(jnp.bfloat16).reshape(item_count, lat_len, local_heads, HEAD_DIM)
    again = masked_scores()
    attention_f = jnp.exp(again - log_total)
    attention_low = attention_f.astype(jnp.bfloat16)
    value_grad = jnp.einsum(
        "ihlk,ilhe->ikhe", attention_low, mixed_grad, preferred_element_type=jnp.float32
    )
    value_grad = value_grad.astype(jnp.bfloat16).reshape(item_count, keys_total, local_width)
    attention_grad = jnp.einsum(
        "ilhe,ikhe->ihlk", mixed_grad, value_heads, preferred_element_type=jnp.float32
    )
    score_grad = attention_f * (
        attention_grad - jnp.sum(attention_grad * attention_f, -1, keepdims=True)
    )
    score_grad = score_grad.astype(jnp.bfloat16)
    query_grad = (
        jnp.einsum("ihlk,ikhe->ilhe", score_grad, key_heads, preferred_element_type=jnp.float32)
        * scale
    )
    query_grad = query_grad.astype(jnp.bfloat16).reshape(item_count, lat_len, local_width)
    key_grad = (
        jnp.einsum("ihlk,ilhe->ikhe", score_grad, query_heads, preferred_element_type=jnp.float32)
        * scale
    )
    key_grad = key_grad.astype(jnp.bfloat16).reshape(item_count, keys_total, local_width)
    kv_grad = jnp.concatenate([key_grad, value_grad], axis=2)
    query_w_grad = jnp.einsum(
        "ild,ile->de", latent_norm, query_grad, preferred_element_type=jnp.float32
    )
    kv_w_grad = jnp.einsum("ikd,ike->de", byte_norm, kv_grad, preferred_element_type=jnp.float32)
    inner_grad = jnp.stack([query_w_grad, kv_w_grad[:, :local_width], kv_w_grad[:, local_width:]])
    latent_norm_part = jnp.einsum(
        "ile,de->ild", query_grad, query_w, preferred_element_type=jnp.float32
    )
    latent_norm_grad = head_total(latent_norm_part)
    latent_pull = jax.vjp(layer_norm, lat_float, norm_vectors[0], norm_vectors[1])[1]
    lat_ln_grad, gain_lat_grad, bias_lat_grad = latent_pull(latent_norm_grad)
    latent_gradient = (residual_grad + lat_ln_grad).astype(jnp.bfloat16)
    rows_here = keys_total // head_count
    row_start = head_index * rows_here
    byte_norm_part = jnp.einsum(
        "ike,de->ikd", kv_grad, key_value_w, preferred_element_type=jnp.float32
    )
    byte_norm_grad = lax.psum_scatter(byte_norm_part, "head", scatter_dimension=1, tiled=True)
    byte_rows = lax.dynamic_slice_in_dim(byte_float, row_start, rows_here, 1)
    byte_pull = jax.vjp(layer_norm, byte_rows, norm_vectors[2], norm_vectors[3])[1]
    byte_ln_grad, gain_key_grad, bias_key_grad = byte_pull(byte_norm_grad)
    byte_gradient = byte_ln_grad.astype(jnp.bfloat16)
    vector_term = jnp.stack(
        [
            gain_lat_grad * first_head,
            bias_lat_grad * first_head,
            gain_key_grad,
            bias_key_grad,
            gain_mlp_grad * first_head,
            bias_mlp_grad * first_head,
            bias_out_grad * first_head,
        ]
    )
    head_rows = (jnp.arange(head_count, dtype=jnp.int32) == head_index).astype(jnp.float32)
    spread_bias = head_rows[:, None] * expand_bias_grad[None, :]
    vector_sum, bias_sum = lax.psum((vector_term, spread_bias), ("dp", "head"))
    bias_local = lax.dynamic_index_in_dim(bias_sum, head_index, 0, keepdims=False)
    small_squares = jnp.sum(vector_sum * vector_sum) + jnp.sum(bias_sum * bias_sum)
    matrix_grads = (inner_grad, output_grad, expand_grad, reduce_grad)
    owned = (
        lax.psum_scatter(matrix_grads[0], "dp", scatter_dimension=1, tiled=True),
        lax.psum_scatter(matrix_grads[1], "dp", scatter_dimension=1, tiled=True),
        lax.psum_scatter(matrix_grads[2], "dp", scatter_dimension=0, tiled=True),
        lax.psum_scatter(matrix_grads[3], "dp", scatter_dimension=1, tiled=True),
    )
    local_squares = sum((jnp.sum(piece * piece) for piece in owned))
    total_squares = lax.psum(local_squares, ("dp", "head"))
    grad_norm = jnp.sqrt(total_squares + small_squares)
    factor = CLIP_RATE * math.sqrt(4 * D * D + 2 * D * FF + FF + 7 * D) / grad_norm
    inner_new = adamw(inner_weight, inner_moment, inner_square, factor * owned[0], 0.03, DECAY)
    outer_new = adamw(output_weight, output_moment, output_square, factor * owned[1], 0.3, DECAY)
    expand_new = adamw(expand_weight, expand_moment, expand_square, factor * owned[2], 0.03, DECAY)
    shrink_new = adamw(reduce_weight, reduce_moment, reduce_square, factor * owned[3], 0.015, DECAY)
    bias_new = adamw(expand_bias, bias_moment, bias_square, factor * bias_local, 0.3, 0.0)
    vector_new = adamw(norm_vectors, vector_moment, vector_square, factor * vector_sum, 0.3, 0.0)
    return (
        block_output,
        latent_gradient,
        byte_gradient,
        inner_new[0],
        inner_new[1],
        inner_new[2],
        outer_new[0],
        outer_new[1],
        outer_new[2],
        expand_new[0],
        expand_new[1],
        expand_new[2],
        shrink_new[0],
        shrink_new[1],
        shrink_new[2],
        bias_new[0],
        bias_new[1],
        bias_new[2],
        vector_new[0],
        vector_new[1],
        vector_new[2],
        grad_norm,
    )


def solution(mesh):
    placed = (
        P("dp", None, None),
        P("dp", None, None),
        P("dp", None, None),
        P("dp"),
        P("dp"),
        P(None, "dp", "head"),
        P(None, "dp", "head"),
        P(None, "dp", "head"),
        P("head", "dp"),
        P("head", "dp"),
        P("head", "dp"),
        P("dp", "head"),
        P("dp", "head"),
        P("dp", "head"),
        P("head", "dp"),
        P("head", "dp"),
        P("head", "dp"),
        P("head"),
        P("head"),
        P("head"),
        P(),
        P(),
        P(),
    )
    return jax.shard_map(
        body,
        mesh=mesh,
        in_specs=placed,
        out_specs=(
            P("dp", None, None),
            P("dp", None, None),
            P("dp", "head", None),
            P(None, "dp", "head"),
            P(None, "dp", "head"),
            P(None, "dp", "head"),
            P("head", "dp"),
            P("head", "dp"),
            P("head", "dp"),
            P("dp", "head"),
            P("dp", "head"),
            P("dp", "head"),
            P("head", "dp"),
            P("head", "dp"),
            P("head", "dp"),
            P("head"),
            P("head"),
            P("head"),
            P(),
            P(),
            P(),
            P(),
        ),
        check_vma=False,
    )
```

profile of v0, /device:TPU:0, one launch (start us, length us, event | category | flops | bytes accessed | tf_op | source)
XLA Modules:
  0.0 782.5 jit_solution(2581162427353771101)
XLA Ops:
  18.0 6.5 multiply_reduce_fusion
  24.5 32.7 %all_gather.13 = bf16[192,768]{0,1:T(8,128)(2,1)S(1)} all-gather(bf16[192,96]{0,1:T(8,128)(2,1)S(1)} %copy.154), channel_id=1, replica_groups=mesh['dp'=8,'head'=4] {'dp'}, dimensions={1}, use_global_device_ids=true | all-gather | bytes 331776 | tf_op jit(solution)/shard_map/all_gather | solution.py:91
  57.3 34.6 %all_gather.12 = bf16[3,768,192]{2,1,0:T(8,128)(2,1)S(1)} all-gather(bf16[3,96,192]{2,1,0:T(8,128)(2,1)S(1)} %convert_element_type.106), channel_id=1, replica_groups=mesh['dp'=8,'head'=4] {'dp'}, dimensions={1}, use_global_device_ids=true | all-gather | bytes 995328 | tf_op jit(solution)/shard_map/all_gather | solution.py:90
  92.0 5.4 add_convert_fusion
  128.3 67.2 %all-reduce.6.cloned.1.call-done = f32[8,128,768]{2,1,0:T(8,128)} async-done(((f32[8,128,768]{2,1,0:T(8,128)}), f32[8,128,768]{2,1,0:T(8,128)}) %all-reduce.6.cloned.1.call-update) | async-done | bytes 3145744 | tf_op jit(solution)/shard_map/psum | solution.py:53
  204.7 8.2 %multiply_convert_fusion.2 = (bf16[8,128,768]{2,1,0:T(8,128)(2,1)}, f32[8,128,768]{2,1,0:T(8,128)}) fusion(f32[8,128,768]{2,1,0:T(8,128)S(1)} %get-tuple-element.216, f32[768]{0:T(1024)S(1)} %copy-done.74, u8[128,768]{1,0:T(8,128)(4,1)S(1)} %get-tuple-element.164, u8[128,768]{1,0:T(8,128)(4,1)S(1)} %get-tuple-element.163), kind=kLoop, calls=%fused_computation.61 | loop fusion | flops 55836672 | bytes 8064000 | tf_op jit(solution)/shard_map/convert_element_type | solution.py:141
  214.2 6.5 convert_reduce_fusion.3
  226.1 4.8 fusion.44
  230.9 61.5 %all-reduce.8.cloned.1.call-done = f32[8,128,768]{2,1,0:T(8,128)} async-done(((f32[8,128,768]{2,1,0:T(8,128)}), f32[8,128,768]{2,1,0:T(8,128)}) %all-reduce.8.cloned.1.call-update) | async-done | bytes 3145744 | tf_op jit(solution)/shard_map/psum | solution.py:53
  301.9 6.9 multiply_reduce_fusion.1
  321.3 5.7 convolution_bitcast_fusion
  327.2 6.7 fusion.34
  338.2 5.1 multiply_convert_fusion.1
  351.7 8.6 %fusion.37 = f32[768,384]{0,1:T(8,128)S(1)} fusion(bf16[8,616,768]{2,0,1:T(8,128)(2,1)} %copy-done.14, bf16[8,616,384]{2,1,0:T(8,128)(2,1)S(1)} %pad_maximum_fusion), kind=kOutput, calls=%fused_computation.83 | convolution fusion | flops 2906652672 | bytes 12533760 | tf_op jit(solution)/shard_map/ikd,ike->de/dot_general | solution.py:194
  372.0 12.6 %fusion.14 = f32[8,616,768]{2,0,1:T(8,128)} fusion(bf16[8,616,384]{2,1,0:T(8,128)(2,1)} %copy-done.11, bf16[768,192]{1,0:T(8,128)(2,1)} %copy-done.23, bf16[768,192]{1,0:T(8,128)(2,1)S(1)} %copy-done.22), kind=kOutput, calls=%fused_computation.40 | convolution fusion | flops 2907832320 | bytes 19513344 | tf_op jit(solution)/shard_map/ike,de->ikd/dot_general | solution.py:205
  390.1 10.2 %copy_convert_fusion = f32[8,616,768]{2,0,1:T(8,128)} fusion(bf16[8,616,768]{2,1,0:T(8,128)(2,1)} %param.24), kind=kLoop, calls=%fused_computation.14 | loop fusion | flops 3784704 | bytes 22708224 | tf_op jit(solution)/shard_map/convert_element_type | solution.py:98
  406.5 30.0 %all-reduce.10.cloned.1.call-done = (f32[8,128,768]{2,1,0:T(8,128)}, f32[8,128,768]{2,1,0:T(8,128)}) async-done(((f32[8,128,768]{2,1,0:T(8,128)}, f32[8,128,768]{2,1,0:T(8,128)}), (f32[8,128,768]{2,1,0:T(8,128)}, f32[8,128,768]{2,1,0:T(8,128)})) %all-reduce.10.cloned.1.call-update) | async-done | bytes 6291472 | tf_op jit(solution)/shard_map/psum | solution.py:53
  447.9 60.7 %reduce-scatter.14.cloned.1.call-done = f32[768,96]{0,1:T(8,128)} async-done(((f32[768,768]{0,1:T(8,128)}), f32[768,96]{0,1:T(8,128)}) %reduce-scatter.14.cloned.1.call-update) | async-done | bytes 294928 | tf_op jit(solution)/shard_map/reduce_scatter | solution.py:234
  510.2 68.5 %reduce-scatter.16.cloned.1.call-done = f32[96,576]{1,0:T(8,128)} async-done(((f32[768,576]{1,0:T(8,128)}), f32[96,576]{1,0:T(8,128)}) %reduce-scatter.16.cloned.1.call-update) | async-done | bytes 221200
  585.0 111.2 %reduce-scatter.10.cloned.1.call-done = f32[8,154,768]{2,0,1:T(8,128)} async-done(((f32[8,616,768]{2,0,1:T(8,128)}), f32[8,154,768]{2,0,1:T(8,128)}) %reduce-scatter.10.cloned.1.call-update) | async-done | bytes 3784720 | tf_op jit(solution)/shard_map/reduce_scatter | solution.py:208
  696.2 5.0 multiply_reduce_fusion.4
  706.5 4.8 multiply_reduce_fusion.2
  716.3 40.1 %all-reduce = (f32[]{:T(128)}, f32[7,768]{1,0:T(8,128)S(1)}, f32[4,768]{1,0:T(4,128)S(1)}) all-reduce(f32[]{:T(128)S(6)} %add.296, f32[7,768]{1,0:T(8,128)S(1)} %stack.32, f32[4,768]{1,0:T(4,128)} %broadcast_multiply_fusion.1), channel_id=1, replica_groups=mesh['dp'=8,'head'=4] {'dp','head'}, use_global_device_ids=true, to_apply=%region_30.31 | all-reduce | flops 8449 | bytes 67592 | tf_op jit(solution)/shard_map/psum | solution.py:237
  766.9 4.9 add_convert_fusion.1
  (311 shorter events, 151.3 us)
Async XLA Ops:
  8.1 187.5 %all-reduce.6.cloned.1.call-start = ((), (), s32[]{:S(2)}) async-start(), calls=%async_computation.5 | async-start | bytes 6291456 | tf_op jit(solution)/shard_map/psum | solution.py:53
  9.9 102.0 %copy-start.49 = (f32[8,128]{1,0:T(8,128)}, f32[8,128]{1,0:T(8,128)S(1)}, u32[]{:S(2)}) copy-start(f32[8,128]{1,0:T(8,128)S(1)} %broadcast_multiply_fusion.9) | copy-start | bytes 12292
  11.9 100.0 %copy-start.62 = (f32[8,128]{1,0:T(8,128)}, f32[8,128]{1,0:T(8,128)S(1)}, u32[]{:S(2)}) copy-start(f32[8,128]{1,0:T(8,128)S(1)} %fusion.69) | copy-start | bytes 12292
  12.5 79.5 %copy-start.47 = (f32[768]{0:T(1024)}, f32[768]{0:T(1024)S(1)}, u32[]{:S(2)}) copy-start(f32[768]{0:T(1024)S(1)} %get-tuple-element.174) | copy-start | bytes 9220
  12.5 99.3 %copy-start.55 = (f32[768]{0:T(1024)}, f32[768]{0:T(1024)S(1)}, u32[]{:S(2)}) copy-start(f32[768]{0:T(1024)S(1)} %get-tuple-element.172) | copy-start | bytes 9220
  12.5 99.3 %copy-start.81 = (f32[768]{0:T(1024)}, f32[768]{0:T(1024)S(1)}, u32[]{:S(2)}) copy-start(f32[768]{0:T(1024)S(1)} %get-tuple-element.171) | copy-start | bytes 9220
  12.5 186.8 %copy-start.60 = (f32[768]{0:T(1024)}, f32[768]{0:T(1024)S(1)}, u32[]{:S(2)}) copy-start(f32[768]{0:T(1024)S(1)} %get-tuple-element.170) | copy-start | bytes 9220
  126.5 72.8 %all-gather.3.cloned.1.call-start = ((), (), s32[]{:S(2)}) async-start(), calls=%async_computation.6 | async-start | bytes 1327104 | tf_op jit(solution)/shard_map/all_gather | solution.py:92
  127.3 86.9 %all-gather.5.cloned.1.call-start = ((), (), s32[]{:S(2)}) async-start(), calls=%async_computation.7 | async-start | bytes 1327104 | tf_op jit(solution)/shard_map/all_gather | solution.py:93
  128.1 164.3 %all-reduce.8.cloned.1.call-start = ((), (), s32[]{:S(2)}) async-start(), calls=%async_computation.8 | async-start | bytes 6291456 | tf_op jit(solution)/shard_map/psum | solution.py:53
  224.9 180.0 %reduce-scatter.18.cloned.1.call-start = ((), (), s32[]{:S(2)}) async-start(), calls=%async_computation.13 | async-start | bytes 884736
  301.9 134.7 %all-reduce.10.cloned.1.call-start = ((), (), s32[]{:S(2)}) async-start(), calls=%async_computation.14 | async-start | bytes 12582912 | tf_op jit(solution)/shard_map/psum | solution.py:53
  316.5 129.7 %reduce-scatter.12.cloned.1.call-start = ((), (), s32[]{:S(2)}) async-start(), calls=%async_computation.10 | async-start | bytes 2654208 | tf_op jit(solution)/shard_map/reduce_scatter | solution.py:233
  321.2 187.4 %reduce-scatter.14.cloned.1.call-start = ((), (), s32[]{:S(2)}) async-start(), calls=%async_computation.11 | async-start | bytes 2654208 | tf_op jit(solution)/shard_map/reduce_scatter | solution.py:234
  327.0 251.7 %reduce-scatter.16.cloned.1.call-start = ((), (), s32[]{:S(2)}) async-start(), calls=%async_computation.12 | async-start | bytes 2211840
  371.8 324.5 %reduce-scatter.10.cloned.1.call-start = ((), (), s32[]{:S(2)}) async-start(), calls=%async_computation.9 | async-start | bytes 18923520 | tf_op jit(solution)/shard_map/reduce_scatter | solution.py:208
  443.1 253.1 %copy-start.48 = (f32[768]{0:T(1024)S(1)}, f32[768]{0:T(1024)}, u32[]{:S(2)}) copy-start(f32[768]{0:T(1024)} %copy-done.47) | copy-start | bytes 9220
  716.2 49.2 %copy-start.35 = (f32[192,96]{1,0:T(8,128)S(1)}, f32[192,96]{1,0:T(8,128)}, u32[]{:S(2)}) copy-start(f32[192,96]{1,0:T(8,128)} %copy-done.34) | copy-start | bytes 221188
  716.2 49.2 %copy-start.39 = (f32[192,96]{1,0:T(8,128)S(1)}, f32[192,96]{1,0:T(8,128)}, u32[]{:S(2)}) copy-start(f32[192,96]{1,0:T(8,128)} %param.31) | copy-start | bytes 221188
  716.3 50.0 %copy-start.75 = (f32[768]{0:T(1024)S(1)}, f32[768]{0:T(1024)}, u32[]{:S(2)}) copy-start(f32[768]{0:T(1024)} %param.40) | copy-start | bytes 9220
  716.3 49.9 %copy-start.79 = (f32[768]{0:T(1024)S(1)}, f32[768]{0:T(1024)}, u32[]{:S(2)}) copy-start(f32[768]{0:T(1024)} %param.41) | copy-start | bytes 9220
  716.3 49.9 %copy-start.80 = (f32[768]{0:T(1024)S(1)}, f32[768]{0:T(1024)}, u32[]{:S(2)}) copy-start(f32[768]{0:T(1024)} %param.42) | copy-start | bytes 9220
  716.3 50.6 %copy-start.36 = (f32[8,154]{0,1:T(8,128)S(1)}, f32[8,154]{0,1:T(8,128)}, u32[]{:S(2)}) copy-start(f32[8,154]{0,1:T(8,128)} %copy.166) | copy-start | bytes 14788
  716.3 50.5 %copy-start.37 = (f32[8,154]{0,1:T(8,128)S(1)}, f32[8,154]{0,1:T(8,128)}, u32[]{:S(2)}) copy-start(f32[8,154]{0,1:T(8,128)} %copy.164) | copy-start | bytes 14788
  (76 other events, 614.8 us)
Sparse Core Ops, SparseCore 0:
  126.6 68.8 all-reduce.5
  225.0 67.3 all-reduce.7
  316.6 119.8 all-reduce.9
Sparse Core Ops, SparseCore 1:
  129.8 41.8 all-gather.2
  174.3 39.8 all-gather.4
  301.9 62.7 reduce-scatter.17
  368.6 68.0 reduce-scatter.11
  440.6 67.9 reduce-scatter.13
  512.5 66.2 reduce-scatter.15
  581.2 114.9 reduce-scatter.9
where the time goes:
time: 788 us; the launch traced here: 783 us
  waiting for transfers between devices  400 us (51%)
  blocking collectives  108 us (14%)
  other arithmetic  99.9 us (13%)
  matrix products  92.2 us (12%)
  local copies, waits for them, and re-layouts  58.3 us (7%)
  between operations  22.6 us (3%)
    psum x3, waiting for transfers between devices, head_total(): return lax.psum(partial_value, 'head')  159 us
    reduce_scatter x1, waiting for transfers between devices, body(): lax.psum_scatter(byte_norm_part, 'head', scatter_dimension=1, tiled=True)  111 us
    unnamed x12, waiting for transfers between devices  68.6 us
    reduce_scatter x1, waiting for transfers between devices, body(): lax.psum_scatter(matrix_grads[3], 'dp', scatter_dimension=1, tiled=True)  60.7 us
    psum x1, blocking collectives, body(): total_squares = lax.psum(local_squares, ('dp', 'head'))  40.1 us
    all_gather x1, blocking collectives, body(): lax.all_gather(inner_weight.astype(jnp.bfloat16), 'dp', axis=1, tiled=True)  34.6 us
    all_gather x1, blocking collectives, body(): lax.all_gather(output_weight.astype(jnp.bfloat16), 'dp', axis=1, tiled=True)  32.7 us
    unnamed x192, local copies, waits for them, and re-layouts  29.1 us
  transfers between devices with their start and end apart: 10, of which 7 were waited for; matrix products, arithmetic and copies ran while one was open for 18% of the time, Pallas kernels for 0%

commit v1 on v0

v1 whole, which is shorter than its diff:
```python
import math

import jax
import jax.numpy as jnp
from jax import lax
from jax.experimental import pallas as pl
from jax.experimental.pallas import tpu as pltpu
from jax.sharding import PartitionSpec as P

D = 768
HEAD_DIM = 64
FF = 3072
PATCHES = 576
STEP = 5

NEG_FILL = -1000000000.0
BETA = 0.5
ADAM_EPS = 1e-08
DECAY = 0.01
CLIP_RATE = 0.01
LN_EPS = 1e-05
SCALE = 1.0 / math.sqrt(HEAD_DIM)
BF = jnp.bfloat16
F32 = jnp.float32
VMEM_LIMIT = 56 * 1024 * 1024


def dot(a, b):
    return lax.dot_general(a, b, (((1,), (0,)), ((), ())), preferred_element_type=F32)


def dot_t(a, b):
    return lax.dot_general(a, b, (((1,), (1,)), ((), ())), preferred_element_type=F32)


def norm_parts(rows):
    centred = rows - jnp.mean(rows, -1, keepdims=True)
    rstd = lax.rsqrt(jnp.mean(centred * centred, -1, keepdims=True) + LN_EPS)
    return centred * rstd, rstd


def norm_back(dy, xhat, rstd, gain):
    scaled = dy * gain
    first = jnp.mean(scaled, -1, keepdims=True)
    second = jnp.mean(scaled * xhat, -1, keepdims=True)
    dx = rstd * (scaled - first - xhat * second)
    return dx, jnp.sum(dy * xhat, 0, keepdims=True), jnp.sum(dy, 0, keepdims=True)


def swap(value, axis, mask):
    size = lax.axis_size(axis)
    return lax.ppermute(value, axis, [(i, i ^ mask) for i in range(size)])


def gather_dp(block):
    size = lax.axis_size("dp")
    index = lax.axis_index("dp")
    held = block[None]
    mask = size // 2
    while mask:
        other = swap(held, "dp", mask)
        bit = (index & mask) != 0
        held = jnp.stack([jnp.where(bit, other, held), jnp.where(bit, held, other)], 1)
        held = held.reshape((-1,) + block.shape)
        mask //= 2
    return held.reshape(-1, block.shape[1])


def scatter_dp(total):
    size = lax.axis_size("dp")
    index = lax.axis_index("dp")
    mask = 1
    while mask < size:
        k, left, rows, cols = total.shape
        pairs = total.reshape(k, left // 2, 2, rows, cols)
        bit = (index & mask) != 0
        away = jnp.where(bit, pairs[:, :, 0], pairs[:, :, 1]).astype(BF)
        kept = jnp.where(bit, pairs[:, :, 1], pairs[:, :, 0])
        total = kept + swap(away, "dp", mask).astype(F32)
        mask *= 2
    return total[:, 0]


def pair_items(mine, core, axis=0):
    other = swap(mine, "head", 1)
    low = core == 0
    return jnp.concatenate([jnp.where(low, mine, other), jnp.where(low, other, mine)], axis)


def adamw(weight, moment, square, gradient, rate, decay_rate):
    moment_new = BETA * moment + (1.0 - BETA) * gradient
    square_new = BETA * square + (1.0 - BETA) * gradient * gradient
    correction = 1.0 - BETA**STEP
    step_dir = moment_new / correction / (jnp.sqrt(square_new / correction) + ADAM_EPS)
    return (weight - rate * (step_dir + decay_rate * weight), moment_new, square_new)


def params(**kw):
    return pltpu.CompilerParams(vmem_limit_bytes=VMEM_LIMIT, **kw)


def cost(flops, nbytes, trans=0):
    return pl.CostEstimate(flops=flops, bytes_accessed=nbytes, transcendentals=trans)


def norm_kernel(info, byte_ref, lat_ref, vec_ref, norm_ref, normt_ref, raw_ref, lat_norm_ref, lat_normt_ref, scr):
    groups, true_rows, pad_rows = 4, byte_ref.shape[1] // 4, norm_ref.shape[1] // 4
    keys = byte_ref.shape[1]
    scr[pl.ds(0, keys), :] = byte_ref[0].astype(F32)
    gain, bias = vec_ref[2:3, :], vec_ref[3:4, :]
    keep = lax.broadcasted_iota(jnp.int32, (pad_rows, 1), 0) < true_rows
    for g in range(groups):
        rows = jnp.where(keep, scr[pl.ds(g * true_rows, pad_rows), :], 0.0)
        xhat, _ = norm_parts(rows)
        normed = jnp.where(keep, xhat * gain + bias, 0.0)
        here = pl.ds(g * pad_rows, pad_rows)
        raw_ref[0, here, :] = rows.astype(BF)
        norm_ref[0, here, :] = normed.astype(BF)
    normt_ref[0] = norm_ref[0].T
    xhat, _ = norm_parts(lat_ref[0].astype(F32))
    lat_norm = (xhat * vec_ref[0:1, :] + vec_ref[1:2, :]).astype(BF)
    lat_norm_ref[0] = lat_norm
    lat_normt_ref[0] = lat_norm.T


def norm_call(info, byte_array, latents, vectors, items, pad_keys):
    _, keys, width = byte_array.shape
    lat_len = latents.shape[1]
    here = lambda i, info: (info[0] * items + i, 0, 0)
    out = lambda i, info: (i, 0, 0)
    return pl.pallas_call(
        norm_kernel,
        grid_spec=pltpu.PrefetchScalarGridSpec(
            num_scalar_prefetch=1,
            grid=(items,),
            in_specs=[
                pl.BlockSpec((1, keys, width), here),
                pl.BlockSpec((1, lat_len, width), here),
                pl.BlockSpec(vectors.shape, lambda i, info: (0, 0)),
            ],
            out_specs=[
                pl.BlockSpec((1, pad_keys, width), out),
                pl.BlockSpec((1, width, pad_keys), out),
                pl.BlockSpec((1, pad_keys, width), out),
                pl.BlockSpec((1, lat_len, width), out),
                pl.BlockSpec((1, width, lat_len), out),
            ],
            scratch_shapes=[pltpu.VMEM((keys + 40, width), F32)],
        ),
        out_shape=[
            jax.ShapeDtypeStruct((items, pad_keys, width), BF),
            jax.ShapeDtypeStruct((items, width, pad_keys), BF),
            jax.ShapeDtypeStruct((items, pad_keys, width), BF),
            jax.ShapeDtypeStruct((items, lat_len, width), BF),
            jax.ShapeDtypeStruct((items, width, lat_len), BF),
        ],
        compiler_params=params(),
        cost_estimate=cost(items * keys * width * 20, items * keys * width * 8),
        name="norms",
    )(info, byte_array, latents, vectors)


def attn_fwd_kernel(info, count_ref, text_ref, norm_ref, lat_ref, wkv_ref, wqo_ref, part_ref, pt_ref, kv_ref, q_ref, mixed_ref):
    items = pl.num_programs(0)
    item = info[0] * items + pl.program_id(0)
    patches, texts = count_ref[item], text_ref[item]
    keys = norm_ref.shape[1]
    pad_rows = keys // 4
    true_rows = info[2]
    row = lax.broadcasted_iota(jnp.int32, (keys, 128), 0)
    group = sum(((row >= pad_rows * g).astype(jnp.int32) for g in range(1, 4)))
    inner = row - group * pad_rows
    slot = inner + group * true_rows
    valid = ((slot < PATCHES) & (slot < patches)) | ((slot >= PATCHES) & (slot - PATCHES < texts))
    valid = valid & (inner < true_rows)
    lane_lo = lax.broadcasted_iota(jnp.int32, (128, 128), 1) < HEAD_DIM
    row_lo = lax.broadcasted_iota(jnp.int32, (128, 128), 0) < HEAD_DIM
    kv_all = dot(norm_ref[0], wkv_ref[...]).astype(BF)
    kv_ref[0] = kv_all
    lat_norm = lat_ref[0]
    total = None
    for p in range(2):
        kv = kv_all[:, p * 384 : (p + 1) * 384]
        base = p * 384
        q = dot(lat_norm, wqo_ref[:, base : base + 256]) * SCALE
        q01, q2 = q[:, :128], jnp.where(lane_lo, q[:, 128:], 0.0).astype(BF)
        q_ref[0, p, :, 0:128] = q01.astype(BF)
        q_ref[0, p, :, 128:256] = q2
        stacked = jnp.concatenate([jnp.where(lane_lo, q01, 0.0), jnp.where(lane_lo, 0.0, q01)], 0).astype(BF)
        first = dot_t(kv[:, 0:128], stacked)
        second = dot_t(kv[:, 256:384], q2)
        pieces = []
        for piece in (first[:, 0:128], first[:, 128:256], second):
            piece = jnp.where(valid, piece, NEG_FILL)
            top = jnp.max(piece, 0, keepdims=True)
            expo = jnp.exp(piece - top)
            pieces.append(expo * (1.0 / jnp.sum(expo, 0, keepdims=True)))
        for h in range(3):
            pt_ref[0, p, :, h * 128 : (h + 1) * 128] = pieces[h]
        low01 = jnp.concatenate([pieces[0].astype(BF), pieces[1].astype(BF)], 1)
        o01 = dot(kv[:, 128:256].T, low01)
        o2 = dot(kv[:, 256:384].T, pieces[2].astype(BF))
        mixed2 = jnp.where(row_lo, 0.0, o2).astype(BF)
        mixed01 = jnp.where(row_lo, o01[:, 0:128], o01[:, 128:256]).astype(BF)
        mixed_ref[0, p, 0:128, :] = mixed2
        mixed_ref[0, p, 128:256, :] = mixed01
        mixed = jnp.concatenate([mixed2.T, mixed01.T], 1)
        add = dot_t(mixed, wqo_ref[:, base + 128 : base + 384])
        total = add if total is None else total + add
    part_ref[0] = total.astype(BF)


def attn_fwd_call(info, counts, texts, norm, lat_norm, wkv, wqo):
    items, keys, width = norm.shape
    lat_len = lat_norm.shape[1]
    out3 = lambda i, *_: (i, 0, 0)
    out4 = lambda i, *_: (i, 0, 0, 0)
    whole = lambda i, *_: (0, 0)
    flops = items * 2 * (keys * width * 768 + lat_len * width * 768 + 4 * keys * lat_len * 384)
    return pl.pallas_call(
        attn_fwd_kernel,
        grid_spec=pltpu.PrefetchScalarGridSpec(
            num_scalar_prefetch=3,
            grid=(items,),
            in_specs=[
                pl.BlockSpec((1, keys, width), out3),
                pl.BlockSpec((1, lat_len, width), out3),
                pl.BlockSpec(wkv.shape, whole),
                pl.BlockSpec(wqo.shape, whole),
            ],
            out_specs=[
                pl.BlockSpec((1, lat_len, width), out3),
                pl.BlockSpec((1, 2, keys, 384), out4),
                pl.BlockSpec((1, keys, 768), out3),
                pl.BlockSpec((1, 2, lat_len, 256), out4),
                pl.BlockSpec((1, 2, 256, lat_len), out4),
            ],
        ),
        out_shape=[
            jax.ShapeDtypeStruct((items, lat_len, width), BF),
            jax.ShapeDtypeStruct((items, 2, keys, 384), F32),
            jax.ShapeDtypeStruct((items, keys, 768), BF),
            jax.ShapeDtypeStruct((items, 2, lat_len, 256), BF),
            jax.ShapeDtypeStruct((items, 2, 256, lat_len), BF),
        ],
        compiler_params=params(),
        cost_estimate=cost(flops, 16 * 1024 * 1024, items * keys * 768),
        name="attn_fwd",
    )(info, counts, texts, norm, lat_norm, wkv, wqo)


def ff_core_kernel(info, lat_ref, cot_ref, own_ref, got_ref, vec_ref, bias_ref, w_own_ref, w_oth_ref,
                   res_ref, normt_ref, cott_ref, hidden_ref, pre_ref, part_ref):
    width = vec_ref.shape[1]
    flat = lambda ref: ref[...].reshape(-1, width).astype(F32)
    residual = flat(lat_ref) + (flat(own_ref) + flat(got_ref))
    res_ref[...] = residual
    xhat, _ = norm_parts(residual)
    normed = (xhat * vec_ref[4:5, :] + vec_ref[5:6, :]).astype(BF)
    cot = cot_ref[...].reshape(-1, width)
    total = None
    step = 256
    for p, w_ref in enumerate((w_own_ref, w_oth_ref)):
        for j in range(768 // step):
            cols = slice(j * step, (j + 1) * step)
            w1 = w_ref[:, j * step : (j + 1) * step]
            pre = dot(normed, w1) + bias_ref[p : p + 1, cols]
            back = dot(cot, w_ref[:, 768 + j * step : 768 + (j + 1) * step])
            cdf = 0.5 + 0.5 * lax.erf(pre * math.sqrt(0.5))
            pdf = jnp.exp(pre * pre * -0.5) * (1.0 / math.sqrt(2.0 * math.pi))
            hidden_ref[p, :, cols] = (pre * cdf).astype(BF)
            grad = (back * (cdf + pre * pdf)).astype(BF)
            pre_ref[p, :, cols] = grad
            add = dot_t(grad, w1)
            total = add if total is None else total + add
    part_ref[...] = total.astype(BF)
    normt_ref[...] = normed.T
    cott_ref[...] = cot.T


def ff_core_call(info, latents, cotangent, own, got, vectors, bias, w_own, w_oth):
    items, lat_len, width = own.shape
    rows = items * lat_len
    half = lambda i, info: (info[0], 0, 0)
    z3 = lambda i, info: (0, 0, 0)
    z2 = lambda i, info: (0, 0)
    return pl.pallas_call(
        ff_core_kernel,
        grid_spec=pltpu.PrefetchScalarGridSpec(
            num_scalar_prefetch=1,
            grid=(1,),
            in_specs=[
                pl.BlockSpec((items, lat_len, width), half),
                pl.BlockSpec((items, lat_len, width), half),
                pl.BlockSpec(own.shape, z3),
                pl.BlockSpec(got.shape, z3),
                pl.BlockSpec(vectors.shape, z2),
                pl.BlockSpec(bias.shape, z2),
                pl.BlockSpec(w_own.shape, z2),
                pl.BlockSpec(w_oth.shape, z2),
            ],
            out_specs=[
                pl.BlockSpec((rows, width), z2),
                pl.BlockSpec((width, rows), z2),
                pl.BlockSpec((width, rows), z2),
                pl.BlockSpec((2, rows, 768), z3),
                pl.BlockSpec((2, rows, 768), z3),
                pl.BlockSpec((rows, width), z2),
            ],
        ),
        out_shape=[
            jax.ShapeDtypeStruct((rows, width), F32),
            jax.ShapeDtypeStruct((width, rows), BF),
            jax.ShapeDtypeStruct((width, rows), BF),
            jax.ShapeDtypeStruct((2, rows, 768), BF),
            jax.ShapeDtypeStruct((2, rows, 768), BF),
            jax.ShapeDtypeStruct((rows, width), BF),
        ],
        compiler_params=params(),
        cost_estimate=cost(6 * rows * width * 1536, 16 * 1024 * 1024, 2 * rows * 1536),
        name="ff_core",
    )(info, latents, cotangent, own, got, vectors, bias, w_own, w_oth)


def ff_grad_kernel(normt_ref, cott_ref, hidden_ref, pre_ref, w2_own_ref, w2_oth_ref,
                   g_own_ref, g_oth_ref, part_ref, bias_ref, cot_sum_ref, acc):
    j = pl.program_id(0)
    normt, cott = normt_ref[...], cott_ref[...]
    total = None
    for p, w_ref in enumerate((w2_own_ref, w2_oth_ref)):
        hidden, pre = hidden_ref[p], pre_ref[p]
        add = dot_t(hidden, w_ref[...])
        total = add if total is None else total + add
        out = (g_own_ref, g_oth_ref)[p]
        out[0] = dot(normt, pre).astype(out.dtype)
        out[1] = dot(cott, hidden).astype(out.dtype)
        bias_ref[p : p + 1, :] = jnp.sum(pre.astype(F32), 0, keepdims=True)

    @pl.when(j == 0)
    def _():
        acc[...] = total
        cot_sum_ref[...] = jnp.sum(cott.astype(F32), 1, keepdims=True)

    @pl.when(j > 0)
    def _():
        acc[...] += total

    part_ref[...] = acc[...].astype(BF)


def ff_grad_call(normt, cott, hidden, pre, w_own, w_oth):
    width, rows = normt.shape
    step = 256
    n = 768 // step
    z2 = lambda j: (0, 0)
    return pl.pallas_call(
        ff_grad_kernel,
        grid=(n,),
        in_specs=[
            pl.BlockSpec((width, rows), z2),
            pl.BlockSpec((width, rows), z2),
            pl.BlockSpec((2, rows, step), lambda j: (0, 0, j)),
            pl.BlockSpec((2, rows, step), lambda j: (0, 0, j)),
            pl.BlockSpec((width, step), lambda j: (0, n + j)),
            pl.BlockSpec((width, step), lambda j: (0, n + j)),
        ],
        out_specs=[
            pl.BlockSpec((2, width, step), lambda j: (0, 0, j)),
            pl.BlockSpec((2, width, step), lambda j: (0, 0, j)),
            pl.BlockSpec((rows, width), z2),
            pl.BlockSpec((2, step), lambda j: (0, j)),
            pl.BlockSpec((width, 1), z2),
        ],
        out_shape=[
            jax.ShapeDtypeStruct((2, width, 768), F32),
            jax.ShapeDtypeStruct((2, width, 768), BF),
            jax.ShapeDtypeStruct((rows, width), BF),
            jax.ShapeDtypeStruct((2, 768), F32),
            jax.ShapeDtypeStruct((width, 1), F32),
        ],
        scratch_shapes=[pltpu.VMEM((rows, width), F32)],
        compiler_params=params(),
        cost_estimate=cost(6 * rows * width * 1536, 16 * 1024 * 1024),
        name="ff_grad",
    )(normt, cott, hidden, pre, w_own, w_oth)


def residual_kernel(info, cot_ref, res_ref, own_ref, got_ref, vec_ref, grad_ref, low_ref, lowt_ref, sums_ref):
    width = vec_ref.shape[1]
    xhat, rstd = norm_parts(res_ref[...])
    dy = own_ref[...].astype(F32) + got_ref[...].astype(F32)
    dx, dgain, dbias = norm_back(dy, xhat, rstd, vec_ref[4:5, :])
    grad = cot_ref[...].reshape(-1, width).astype(F32) + dx
    grad_ref[...] = grad
    low = grad.astype(BF)
    low_ref[...] = low
    lowt_ref[...] = low.T
    sums_ref[0:1, :] = dgain
    sums_ref[1:2, :] = dbias


def residual_call(info, cotangent, residual, own, got, vectors):
    rows, width = residual.shape
    lat_len = cotangent.shape[1]
    items = rows // lat_len
    z2 = lambda i, info: (0, 0)
    return pl.pallas_call(
        residual_kernel,
        grid_spec=pltpu.PrefetchScalarGridSpec(
            num_scalar_prefetch=1,
            grid=(1,),
            in_specs=[
                pl.BlockSpec((items, lat_len, width), lambda i, info: (info[0], 0, 0)),
                pl.BlockSpec((rows, width), z2),
                pl.BlockSpec((rows, width), z2),
                pl.BlockSpec((rows, width), z2),
                pl.BlockSpec(vectors.shape, z2),
            ],
            out_specs=[
                pl.BlockSpec((rows, width), z2),
                pl.BlockSpec((rows, width), z2),
                pl.BlockSpec((width, rows), z2),
                pl.BlockSpec((2, width), z2),
            ],
        ),
        out_shape=[
            jax.ShapeDtypeStruct((rows, width), F32),
            jax.ShapeDtypeStruct((rows, width), BF),
            jax.ShapeDtypeStruct((width, rows), BF),
            jax.ShapeDtypeStruct((2, width), F32),
        ],
        compiler_params=params(),
        cost_estimate=cost(rows * width * 20, 10 * 1024 * 1024),
        name="residual_back",
    )(info, cotangent, residual, own, got, vectors)


def attn_bwd_kernel(low_ref, lowt_ref, pt_ref, kv_ref, q_ref, mixed_ref, normt_ref, lat_normt_ref, wqo_ref,
                    lat_part_ref, dkv_ref, g_own_ref, g_oth_ref, gkv, gqo):
    i = pl.program_id(0)

    @pl.when(i == 0)
    def _():
        gkv[...] = jnp.zeros_like(gkv)
        gqo[...] = jnp.zeros_like(gqo)

    lane_lo = lax.broadcasted_iota(jnp.int32, (128, 128), 1) < HEAD_DIM
    row_lo = lax.broadcasted_iota(jnp.int32, (128, 128), 0) < HEAD_DIM
    low = low_ref[...]
    both = jnp.concatenate([lat_normt_ref[0], lowt_ref[...]], 1)
    none = jnp.zeros((128, 128), BF)
    total = None
    for p in range(2):
        base = p * 384
        kv = kv_ref[0, :, base : base + 384]
        mixed_grad = dot(low, wqo_ref[:, base + 128 : base + 384])
        mg2 = jnp.where(lane_lo, 0.0, mixed_grad[:, 0:128]).astype(BF)
        mg01 = mixed_grad[:, 128:256]
        mg01 = jnp.concatenate([jnp.where(lane_lo, mg01, 0.0), jnp.where(lane_lo, 0.0, mg01)], 0).astype(BF)
        first = dot_t(kv[:, 128:256], mg01)
        second = dot_t(kv[:, 256:384], mg2)
        probs, scores = [], []
        for h, piece in enumerate((first[:, 0:128], first[:, 128:256], second)):
            prob = pt_ref[0, p, :, h * 128 : (h + 1) * 128]
            inner = jnp.sum(piece * prob, 0, keepdims=True)
            scores.append((prob * (piece - inner)).astype(BF))
            probs.append(prob.astype(BF))
        q01 = q_ref[0, p, :, 0:128].astype(F32)
        q01 = jnp.concatenate([jnp.where(lane_lo, q01, 0.0), jnp.where(lane_lo, 0.0, q01)], 0).astype(BF)
        q2 = q_ref[0, p, :, 128:256]
        ds01 = jnp.concatenate(scores[:2], 1)
        dkv_ref[0, :, base : base + 128] = dot(ds01, q01).astype(BF)
        dkv_ref[0, :, base + 128 : base + 256] = dot(jnp.concatenate(probs[:2], 1), mg01).astype(BF)
        dkv_ref[0, :, base + 256 : base + 384] = dot(
            jnp.concatenate([scores[2], probs[2]], 1), jnp.concatenate([q2, mg2], 0)
        ).astype(BF)
        dq01 = dot(kv[:, 0:128].T, ds01)
        dq2 = dot(kv[:, 256:384].T, scores[2])
        dq01 = (jnp.where(row_lo, dq01[:, 0:128], dq01[:, 128:256]) * SCALE).astype(BF)
        dq2 = (jnp.where(row_lo, dq2, 0.0) * SCALE).astype(BF)
        add = dot_t(jnp.concatenate([dq01.T, dq2.T], 1), wqo_ref[:, base : base + 256])
        total = add if total is None else total + add
        right = jnp.concatenate(
            [
                jnp.concatenate([dq01, none], 1),
                jnp.concatenate([dq2, mixed_ref[0, p, 0:128, :]], 1),
                jnp.concatenate([none, mixed_ref[0, p, 128:256, :]], 1),
            ],
            0,
        )
        gqo[:, base : base + 384] += dot_t(both, right)
    lat_part_ref[...] = total.astype(BF)
    gkv[...] += dot(normt_ref[0], dkv_ref[0])

    @pl.when(i == pl.num_programs(0) - 1)
    def _():
        g_own_ref[:, 0:384] = gkv[:, 0:384]
        g_own_ref[:, 384:768] = gqo[:, 0:384]
        g_oth_ref[:, 0:384] = gkv[:, 384:768].astype(BF)
        g_oth_ref[:, 384:768] = gqo[:, 384:768].astype(BF)


def attn_bwd_call(low, lowt, pt, kv, q, mixed, normt, lat_normt, wqo):
    items, keys, _ = kv.shape
    width = lowt.shape[0]
    lat_len = q.shape[2]
    three = lambda i: (i, 0, 0)
    four = lambda i: (i, 0, 0, 0)
    z2 = lambda i: (0, 0)
    flops = items * 2 * (keys * width * 768 + 3 * lat_len * width * 768 + 10 * keys * lat_len * 384)
    return pl.pallas_call(
        attn_bwd_kernel,
        grid=(items,),
        in_specs=[
            pl.BlockSpec((lat_len, width), lambda i: (i, 0)),
            pl.BlockSpec((width, lat_len), lambda i: (0, i)),
            pl.BlockSpec((1, 2, keys, 384), four),
            pl.BlockSpec((1, keys, 768), three),
            pl.BlockSpec((1, 2, lat_len, 256), four),
            pl.BlockSpec((1, 2, 256, lat_len), four),
            pl.BlockSpec((1, width, keys), three),
            pl.BlockSpec((1, width, lat_len), three),
            pl.BlockSpec(wqo.shape, z2),
        ],
        out_specs=[
            pl.BlockSpec((lat_len, width), lambda i: (i, 0)),
            pl.BlockSpec((1, keys, 768), three),
            pl.BlockSpec((width, 768), z2),
            pl.BlockSpec((width, 768), z2),
        ],
        out_shape=[
            jax.ShapeDtypeStruct((items * lat_len, width), BF),
            jax.ShapeDtypeStruct((items, keys, 768), BF),
            jax.ShapeDtypeStruct((width, 768), F32),
            jax.ShapeDtypeStruct((width, 768), BF),
        ],
        scratch_shapes=[pltpu.VMEM((width, 768), F32), pltpu.VMEM((width, 768), F32)],
        compiler_params=params(),
        cost_estimate=cost(flops, 24 * 1024 * 1024),
        name="attn_bwd",
    )(low, lowt, pt, kv, q, mixed, normt, lat_normt, wqo)


def latent_kernel(info, lat_ref, grad_ref, own_ref, got_ref, vec_ref, out_ref, sums_ref):
    width = vec_ref.shape[1]
    xhat, rstd = norm_parts(lat_ref[...].reshape(-1, width).astype(F32))
    dy = own_ref[...].astype(F32) + got_ref[...].astype(F32)
    dx, dgain, dbias = norm_back(dy, xhat, rstd, vec_ref[0:1, :])
    out_ref[...] = (grad_ref[...] + dx).astype(BF).reshape(out_ref.shape)
    sums_ref[0:1, :] = dgain
    sums_ref[1:2, :] = dbias


def latent_call(info, latents, grad, own, got, vectors):
    rows, width = grad.shape
    lat_len = latents.shape[1]
    items = rows // lat_len
    z2 = lambda i, info: (0, 0)
    return pl.pallas_call(
        latent_kernel,
        grid_spec=pltpu.PrefetchScalarGridSpec(
            num_scalar_prefetch=1,
            grid=(1,),
            in_specs=[
                pl.BlockSpec((items, lat_len, width), lambda i, info: (info[0], 0, 0)),
                pl.BlockSpec((rows, width), z2),
                pl.BlockSpec((rows, width), z2),
                pl.BlockSpec((rows, width), z2),
                pl.BlockSpec(vectors.shape, z2),
            ],
            out_specs=[
                pl.BlockSpec((items, lat_len, width), lambda i, info: (0, 0, 0)),
                pl.BlockSpec((2, width), z2),
            ],
        ),
        out_shape=[
            jax.ShapeDtypeStruct((items, lat_len, width), BF),
            jax.ShapeDtypeStruct((2, width), F32),
        ],
        compiler_params=params(),
        cost_estimate=cost(rows * width * 20, 6 * 1024 * 1024),
        name="latent_back",
    )(info, latents, grad, own, got, vectors)


def byte_send_kernel(info, dkv_ref, wkv_ref, out_ref):
    out_ref[0] = dot_t(dkv_ref[0], wkv_ref[...]).astype(BF)


def byte_send_call(info, dkv, wkv):
    items, keys, _ = dkv.shape
    width = wkv.shape[0]
    half = keys // 2
    return pl.pallas_call(
        byte_send_kernel,
        grid_spec=pltpu.PrefetchScalarGridSpec(
            num_scalar_prefetch=1,
            grid=(items,),
            in_specs=[
                pl.BlockSpec((1, half, 768), lambda i, info: (i, 1 - info[1], 0)),
                pl.BlockSpec(wkv.shape, lambda i, info: (0, 0)),
            ],
            out_specs=pl.BlockSpec((1, half, width), lambda i, info: (i, 0, 0)),
        ),
        out_shape=jax.ShapeDtypeStruct((items, half, width), BF),
        compiler_params=params(),
        cost_estimate=cost(items * half * width * 768 * 2, 6 * 1024 * 1024),
        name="byte_send",
    )(info, dkv, wkv)


def byte_back_kernel(info, dkv_ref, got_ref, raw_ref, wkv_ref, vec_ref, own_ref, oth_ref, sums_ref):
    i = pl.program_id(0)
    dy = dot_t(dkv_ref[0], wkv_ref[...]) + got_ref[0].astype(F32)
    xhat, rstd = norm_parts(raw_ref[0].astype(F32))
    dx, dgain, dbias = norm_back(dy, xhat, rstd, vec_ref[2:3, :])
    quarter = dx.shape[0] // 2

    @pl.when(info[0] == 0)
    def _():
        own_ref[0] = dx[:quarter].astype(BF)
        oth_ref[0] = dx[quarter:].astype(BF)

    @pl.when(info[0] != 0)
    def _():
        own_ref[0] = dx[quarter:].astype(BF)
        oth_ref[0] = dx[:quarter].astype(BF)

    @pl.when(i == 0)
    def _():
        sums_ref[...] = jnp.zeros_like(sums_ref)

    sums_ref[0:1, :] += dgain
    sums_ref[1:2, :] += dbias


def byte_back_call(info, dkv, got, raw, wkv, vectors):
    items, keys, _ = dkv.shape
    width = wkv.shape[0]
    half = keys // 2
    mine = lambda i, info: (i, info[1], 0)
    out = lambda i, info: (i, 0, 0)
    z2 = lambda i, info: (0, 0)
    return pl.pallas_call(
        byte_back_kernel,
        grid_spec=pltpu.PrefetchScalarGridSpec(
            num_scalar_prefetch=1,
            grid=(items,),
            in_specs=[
                pl.BlockSpec((1, half, 768), mine),
                pl.BlockSpec((1, half, width), out),
                pl.BlockSpec((1, half, width), mine),
                pl.BlockSpec(wkv.shape, z2),
                pl.BlockSpec(vectors.shape, z2),
            ],
            out_specs=[
                pl.BlockSpec((1, half // 2, width), out),
                pl.BlockSpec((1, half // 2, width), out),
                pl.BlockSpec((2, width), z2),
            ],
        ),
        out_shape=[
            jax.ShapeDtypeStruct((items, half // 2, width), BF),
            jax.ShapeDtypeStruct((items, half // 2, width), BF),
            jax.ShapeDtypeStruct((2, width), F32),
        ],
        compiler_params=params(),
        cost_estimate=cost(items * half * width * 768 * 2, 8 * 1024 * 1024),
        name="byte_back",
    )(info, dkv, got, raw, wkv, vectors)


def body(
    latents, byte_array, cotangent, patch_count, text_len,
    inner_weight, inner_moment, inner_square,
    output_weight, output_moment, output_square,
    expand_weight, expand_moment, expand_square,
    reduce_weight, reduce_moment, reduce_square,
    expand_bias, bias_moment, bias_square,
    norm_vectors, vector_moment, vector_square,
):
    item_count, lat_len, width = latents.shape
    keys = byte_array.shape[1]
    items = item_count // 2
    n = lax.axis_size("dp")
    head = lax.axis_index("head")
    core, xside = head & 1, head >> 1
    true_rows = keys // lax.axis_size("head")
    pad_rows = -(-true_rows // 32) * 32
    pad_keys = 4 * pad_rows
    info = jnp.stack([core, xside, jnp.int32(true_rows)]).astype(jnp.int32)

    low_inner = inner_weight.astype(BF)
    wq, wk, wv = low_inner[0], low_inner[1], low_inner[2]
    wo = output_weight.astype(BF).T
    pack = jnp.concatenate(
        [wk[:, :128], wv[:, :128], wk[:, 128:], wv[:, 128:], wq[:, :128], wq[:, 128:], wo[:, 128:], wo[:, :128]], 1
    )
    own_w = gather_dp(pack)
    oth_w = swap(own_w, "head", 1)
    wkv = jnp.concatenate([own_w[:, :384], oth_w[:, :384]], 1)
    wqo = jnp.concatenate([own_w[:, 384:], oth_w[:, 384:]], 1)
    ff_pack = jnp.concatenate([expand_weight.astype(BF), reduce_weight.astype(BF).T], 1)
    ff_own = lax.all_gather(ff_pack, "dp", axis=0, tiled=True)
    ff_oth = swap(ff_own, "head", 1)
    bias_both = jnp.stack([expand_bias, swap(expand_bias, "head", 1)])

    norm, normt, raw, lat_norm, lat_normt = norm_call(info, byte_array, latents, norm_vectors, items, pad_keys)
    attn_part, pt, kv, q, mixed = attn_fwd_call(info, patch_count, text_len, norm, lat_norm, wkv, wqo)
    attn_got = swap(attn_part, "head", 2)

    residual, mlp_normt, cott, hidden, pre_grad, norm_part = ff_core_call(
        info, latents, cotangent, attn_part, attn_got, norm_vectors, bias_both, ff_own, ff_oth
    )
    norm_got = swap(norm_part, "head", 2)
    g_ff, g_ff_oth, mlp_part, bias_part, cot_sum = ff_grad_call(mlp_normt, cott, hidden, pre_grad, ff_own, ff_oth)
    mlp_got = swap(mlp_part, "head", 2)
    block_mine = residual + (mlp_part.astype(F32) + mlp_got.astype(F32)) + norm_vectors[6]
    block_output = pair_items(block_mine.astype(BF).reshape(items, lat_len, width), core)

    residual_grad, low, lowt, mlp_sums = residual_call(info, cotangent, residual, norm_part, norm_got, norm_vectors)
    lat_part, dkv, g_attn, g_attn_oth = attn_bwd_call(low, lowt, pt, kv, q, mixed, normt, lat_normt, wqo)

    byte_got = swap(byte_send_call(info, dkv, wkv), "head", 2)
    byte_own, byte_oth, byte_sums = byte_back_call(info, dkv, byte_got, raw, wkv, norm_vectors)
    byte_recv = swap(byte_oth, "head", 1)
    is_low = core == 0
    byte_gradient = jnp.concatenate(
        [jnp.where(is_low, byte_own, byte_recv), jnp.where(is_low, byte_recv, byte_own)], 0
    )[:, :true_rows]

    lat_got = swap(lat_part, "head", 2)
    lat_mine, lat_sums = latent_call(info, latents, residual_grad, lat_part, lat_got, norm_vectors)
    latent_gradient = pair_items(lat_mine, core)

    g_ff = scatter_dp((g_ff + swap(g_ff_oth, "head", 1).astype(F32)).reshape(2, n, width // n, 768))
    g_attn = scatter_dp((g_attn + swap(g_attn_oth, "head", 1).astype(F32)).reshape(1, n, width // n, 768))[0]
    bias_own = bias_part[0] + swap(bias_part[1], "head", 1)
    expand_g, reduce_gt = g_ff[0], g_ff[1]
    once = (xside == 0).astype(F32)
    squares = jnp.sum(g_ff * g_ff) + jnp.sum(g_attn * g_attn)
    vec = jnp.concatenate(
        [lat_sums * once, byte_sums, mlp_sums * once, (cot_sum * once).reshape(1, width)], 0
    )
    load = jnp.concatenate([vec, bias_own[None], jnp.full((1, width), squares, F32)], 0)
    mask = n // 2
    while mask:
        load = load + swap(load, "dp", mask)
        mask //= 2
    bias_sum = load[7]
    squares = load[8:9] + jnp.sum(bias_sum * bias_sum)
    load = jnp.concatenate([load[:7], squares], 0)
    load = load + swap(load, "head", 1)
    load = load + swap(load, "head", 2)
    vector_sum = load[:7]
    grad_norm = jnp.sqrt(load[7, 0] + jnp.sum(vector_sum * vector_sum))
    factor = CLIP_RATE * math.sqrt(4 * D * D + 2 * D * FF + FF + 7 * D) / grad_norm

    g_k = jnp.concatenate([g_attn[:, 0:128], g_attn[:, 256:320]], 1)
    g_v = jnp.concatenate([g_attn[:, 128:256], g_attn[:, 320:384]], 1)
    g_q = jnp.concatenate([g_attn[:, 384:512], g_attn[:, 512:576]], 1)
    g_o = jnp.concatenate([g_attn[:, 640:768], g_attn[:, 576:640]], 1).T
    inner_new = adamw(inner_weight, inner_moment, inner_square, factor * jnp.stack([g_q, g_k, g_v]), 0.03, DECAY)
    outer_new = adamw(output_weight, output_moment, output_square, factor * g_o, 0.3, DECAY)
    expand_new = adamw(expand_weight, expand_moment, expand_square, factor * expand_g, 0.03, DECAY)
    shrink_new = adamw(reduce_weight, reduce_moment, reduce_square, factor * reduce_gt.T, 0.015, DECAY)
    bias_new = adamw(expand_bias, bias_moment, bias_square, factor * bias_sum, 0.3, 0.0)
    vector_new = adamw(norm_vectors, vector_moment, vector_square, factor * vector_sum, 0.3, 0.0)
    return (
        block_output, latent_gradient, byte_gradient,
        *inner_new, *outer_new, *expand_new, *shrink_new, *bias_new, *vector_new, grad_norm,
    )


def solution(mesh):
    rows, cols = P("dp", "head"), P("head", "dp")
    inner, items = P(None, "dp", "head"), P("dp", None, None)
    weights = (inner,) * 3 + (cols,) * 3 + (rows,) * 3 + (cols,) * 3 + (P("head"),) * 3 + (P(),) * 3
    return jax.shard_map(
        body,
        mesh=mesh,
        in_specs=(items, items, items, P("dp"), P("dp")) + weights,
        out_specs=(items, items, P("dp", "head", None)) + weights + (P(),),
        check_vma=False,
    )
```

time: 788 us -> 336 us (0.43)
  waiting for transfers between devices: 400 us -> 149 us
  blocking collectives: 108 us -> 0 us
  Pallas kernels: 0 us -> 95.5 us
  matrix products: 92.2 us -> 0 us
  other arithmetic: 99.9 us -> 23.9 us
  local copies, waits for them, and re-layouts: 58.3 us -> 15.5 us
  starting transfers between devices: 1.43 us -> 32.1 us
    reduce_scatter x3 -> x0, waiting for transfers between devices: 172 us -> none  [the longest x1 111 us: body(): lax.psum_scatter(byte_norm_part, 'head', scatter_dimension=1, tiled=True)]
    psum x3 -> x0, waiting for transfers between devices: 159 us -> none  [head_total(): return lax.psum(partial_value, 'head')]
    ppermute x0 -> x28, waiting for transfers between devices: none -> 130 us  [swap(): return lax.ppermute(value, axis, [(i, i ^ mask) for i in range(size)])]
    pallas_call x0 -> x9, Pallas kernels: none -> 95.5 us  [the longest x1 23.7 us: attn_bwd_call(): pl.pallas_call(attn_bwd_kernel, grid=(items,), in_specs=[pl.BlockSpec((la...]
    dot_general x21 -> x0, matrix products: 92.2 us -> none  [the longest x1 12.6 us: body(): jnp.einsum('ike,de->ikd', kv_grad, key_value_w, preferred_element_type=jn...]
    unnamed x12 -> x1, waiting for transfers between devices: 68.6 us -> 0.02 us
    all_gather x2 -> x0, blocking collectives: 67.4 us -> none  [the longest x1 34.6 us: body(): lax.all_gather(inner_weight.astype(jnp.bfloat16), 'dp', axis=1, tiled=True)]
    reduce_sum x21 -> x4, other arithmetic: 50.3 us -> 2.64 us  [the longest x2 1.43 us: body(): squares = jnp.sum(g_ff * g_ff) + jnp.sum(g_attn * g_attn)]
  transfers between devices with their start and end apart: 10 -> 29, of which waited for: 7 -> 19; matrix products, arithmetic and copies ran while one was open for 18% -> 7% of each run, Pallas kernels for 0% -> 25%
where the time goes in v1:
time: 336 us; the launch traced here: 335 us
  waiting for transfers between devices  149 us (44%)
  Pallas kernels  95.5 us (28%)
  starting transfers between devices  32.1 us (10%)
  other arithmetic  23.9 us (7%)
  between operations  18.6 us (6%)
  local copies, waits for them, and re-layouts  15.5 us (5%)
    ppermute x28, waiting for transfers between devices, swap(): return lax.ppermute(value, axis, [(i, i ^ mask) for i in range(size)])  130 us
    ppermute x28, starting transfers between devices, swap(): return lax.ppermute(value, axis, [(i, i ^ mask) for i in range(size)])  32 us
    pallas_call x1, Pallas kernels, attn_bwd_call(): pl.pallas_call(attn_bwd_kernel, grid=(items,), in_specs=[pl.BlockSpec((la...  23.7 us
    all_gather x1, waiting for transfers between devices, body(): ff_own = lax.all_gather(ff_pack, 'dp', axis=0, tiled=True)  18.8 us
    pallas_call x1, Pallas kernels, attn_fwd_call(): pl.pallas_call(attn_fwd_kernel, grid_spec=pltpu.PrefetchScalarGridSpec(nu...  16.6 us
    unnamed x87, local copies, waits for them, and re-layouts  11.7 us
    pallas_call x1, Pallas kernels, ff_core_call(): pl.pallas_call(ff_core_kernel, grid_spec=pltpu.PrefetchScalarGridSpec(num...  11.5 us
    pallas_call x1, Pallas kernels, ff_grad_call(): pl.pallas_call(ff_grad_kernel, grid=(n,), in_specs=[pl.BlockSpec((width,...  9.49 us
  transfers between devices with their start and end apart: 29, of which 19 were waited for; matrix products, arithmetic and copies ran while one was open for 7% of the time, Pallas kernels for 25%

profile of v1, /device:TPU:0, one launch (start us, length us, event | category | flops | bytes accessed | tf_op | source)
XLA Modules:
  0.0 334.7 jit_solution(6888425750421211069)
XLA Ops:
  14.5 7.0 %collective-permute-done = bf16[1,96,768]{2,1,0:T(8,128)(2,1)S(1)} collective-permute-done((bf16[1,96,768]{2,1,0:T(8,128)(2,1)S(1)}, bf16[1,96,768]{2,1,0:T(8,128)(2,1)S(1)}, u32[]{:S(2)}, u32[]{:S(2)}) %collective-permute-start) | collective-permute-done | bytes 147488 | tf_op jit(solution)/shard_map/ppermute | solution.py:52
  22.3 14.6 %collective-permute-done.1 = bf16[2,96,768]{2,1,0:T(8,128)(2,1)S(1)} collective-permute-done((bf16[2,96,768]{2,1,0:T(8,128)(2,1)S(1)}, bf16[2,96,768]{2,1,0:T(8,128)(2,1)S(1)}, u32[]{:S(2)}, u32[]{:S(2)}) %collective-permute-start.1) | collective-permute-done | bytes 294944 | tf_op jit(solution)/shard_map/ppermute | solution.py:52
  38.2 16.7 %collective-permute-done.2 = bf16[4,96,768]{2,1,0:T(8,128)(2,1)S(1)} collective-permute-done((bf16[4,96,768]{2,1,0:T(8,128)(2,1)S(1)}, bf16[4,96,768]{2,1,0:T(8,128)(2,1)S(1)}, u32[]{:S(2)}, u32[]{:S(2)}) %collective-permute-start.2) | collective-permute-done | bytes 589856 | tf_op jit(solution)/shard_map/ppermute | solution.py:52
  55.3 18.8 %all-gather.2.cloned.1.call-done.w_own_ref.w2_own_ref = bf16[768,1536]{1,0:T(8,128)(2,1)} async-done(((bf16[96,1536]{1,0:T(8,128)(2,1)}), bf16[768,1536]{1,0:T(8,128)(2,1)}) %all-gather.2.cloned.1.call-update) | async-done | bytes 2359312 | tf_op jit(solution)/shard_map/all_gather | solution.py:704
  74.6 9.4 %norms.1 = (bf16[4,640,768]{2,1,0:T(8,128)(2,1)}, bf16[4,768,640]{2,1,0:T(8,128)(2,1)}, bf16[4,640,768]{2,1,0:T(8,128)(2,1)}, bf16[4,128,768]{2,1,0:T(8,128)(2,1)}, bf16[4,768,128]{2,1,0:T(8,128)(2,1)}) custom-call(s32[3]{0:T(128)} %pad_add_fusion.info, bf16[8,616,768]{2,1,0:T(8,128)(2,1)} %byte_ref.1, bf16[8,128,768]{2,1,0:T(8,128)(2,1)} %lat_ref.5, ...), custom_call_target="tpu_custom_call" | custom-call | flops 37847040 | bytes 15138816 | tf_op jit(solution)/shard_map/norms/pallas_call | solution.py:131
  85.9 16.6 %attn_fwd.1 = (bf16[4,128,768]{2,1,0:T(8,128)(2,1)}, f32[4,2,640,384]{3,2,1,0:T(8,128)}, bf16[4,640,768]{2,1,0:T(8,128)(2,1)}, bf16[4,2,128,256]{3,2,1,0:T(8,128)(2,1)}, bf16[4,2,256,128]{3,2,1,0:T(8,128)(2,1)}) custom-call(s32[3]{0:T(128)} %pad_add_fusion.info, s32[8]{0:T(128)} %count_ref.1, s32[8]{0:T(128)} %text_ref.1, ...), custom_call_target="tpu_custom_call" | custom-call | flops 4630511616 | bytes 16777216 | tf_op jit(solution)/shard_map/attn_fwd/pallas_call | solution.py:220
  105.9 16.8 %collective-permute-done.4.got_ref = bf16[4,128,768]{2,1,0:T(8,128)(2,1)S(1)} collective-permute-done((bf16[4,128,768]{2,1,0:T(8,128)(2,1)}, bf16[4,128,768]{2,1,0:T(8,128)(2,1)S(1)}, u32[]{:S(2)}, u32[]{:S(2)}) %collective-permute-start.4) | collective-permute-done | bytes 786464 | tf_op jit(solution)/shard_map/ppermute | solution.py:52
  123.6 11.5 %ff_core.1 = (f32[512,768]{1,0:T(8,128)}, bf16[768,512]{1,0:T(8,128)(2,1)}, bf16[768,512]{1,0:T(8,128)(2,1)}, bf16[2,512,768]{2,1,0:T(8,128)(2,1)}, bf16[2,512,7...) custom-call(s32[3]{0:T(128)} %pad_add_fusion.info, bf16[8,128,768]{2,1,0:T(8,128)(2,1)} %lat_ref.5, ...), custom_call_target="tpu_custom_call" | custom-call | flops 3623878656 | bytes 16777216 | tf_op jit(solution)/shard_map/ff_core/pallas_call | solution.py:287
  138.2 9.5 %ff_grad.1 = (f32[2,768,768]{2,1,0:T(8,128)}, bf16[2,768,768]{2,1,0:T(8,128)(2,1)}, bf16[512,768]{1,0:T(8,128)(2,1)}, f32[2,768]{1,0:T(2,128)}, f32[768,1]{1,0:T(8,128)}) custom-call(bf16[768,512]{1,0:T(8,128)(2,1)} %get-tuple-element.60.normt_ref, bf16[768,512]{1,0:T(8,128)(2,1)} %get-tuple-element.61.cott_ref, ...), custom_call_target="tpu_custom_call" | custom-call | flops 3623878656 | bytes 16777216 | tf_op jit(solution)/shard_map/ff_grad/pallas_call | solution.py:356
  149.0 6.8 %collective-permute-done.9.got_ref = bf16[512,768]{1,0:T(8,128)(2,1)S(1)} collective-permute-done((bf16[512,768]{1,0:T(8,128)(2,1)}, bf16[512,768]{1,0:T(8,128)(2,1)S(1)}, u32[]{:S(2)}, u32[]{:S(2)}) %collective-permute-start.9) | collective-permute-done | bytes 786464 | tf_op jit(solution)/shard_map/ppermute | solution.py:52
  156.6 5.8 %residual_back.1 = (f32[512,768]{1,0:T(8,128)}, bf16[512,768]{1,0:T(8,128)(2,1)}, bf16[768,512]{1,0:T(8,128)(2,1)}, f32[2,768]{1,0:T(2,128)}) custom-call(s32[3]{0:T(128)} %pad_add_fusion.info, bf16[8,128,768]{2,1,0:T(8,128)(2,1)} %cot_ref.3, f32[512,768]{1,0:T(8,128)} %get-tuple-element.59.res_ref, bf16[512,768]{1,0:T(8,128)(2,1)} %get-tuple-element.65.own_ref, ...), custom_call_target="tpu_custom_call" | custom-call | flops 7864320 | bytes 10485760 | tf_op jit(solution)/shard_map/residual_back/pallas_call | solution.py:407
  162.4 23.7 %attn_bwd.1 = (bf16[512,768]{1,0:T(8,128)(2,1)}, bf16[4,640,768]{2,1,0:T(8,128)(2,1)}, f32[768,768]{1,0:T(8,128)}, bf16[768,768]{1,0:T(8,128)(2,1)}) custom-call(bf16[512,768]{1,0:T(8,128)(2,1)} %get-tuple-element.67.low_ref, bf16[768,512]{1,0:T(8,128)(2,1)} %get-tuple-element.68.lowt_ref, f32[4,2,640,384]{3,2,1,0:T(8,128)} %get-tuple-element.69.pt_ref, ...), custom_call_target="tpu_custom_call" | custom-call | flops 7348420608 | bytes 25165824 | tf_op jit(solution)/shard_map/attn_bwd/pallas_call | solution.py:511
  191.7 6.1 %byte_send.1 = bf16[4,320,768]{2,1,0:T(8,128)(2,1)} custom-call(s32[3]{0:T(128)} %pad_add_fusion.info, bf16[4,640,768]{2,1,0:T(8,128)(2,1)} %get-tuple-element.77.dkv_ref, bf16[768,768]{1,0:T(8,128)(2,1)} %get-tuple-element.183.wkv_ref), custom_call_target="tpu_custom_call" | custom-call | flops 1509949440 | bytes 6291456 | tf_op jit(solution)/shard_map/byte_send/pallas_call | solution.py:594
  198.2 8.6 %collective-permute-done.10.got_ref = bf16[512,768]{1,0:T(8,128)(2,1)S(1)} collective-permute-done((bf16[512,768]{1,0:T(8,128)(2,1)}, bf16[512,768]{1,0:T(8,128)(2,1)S(1)}, u32[]{:S(2)}, u32[]{:S(2)}) %collective-permute-start.10) | collective-permute-done | bytes 786464 | tf_op jit(solution)/shard_map/ppermute | solution.py:52
  207.7 4.9 %latent_back.1 = (bf16[4,128,768]{2,1,0:T(8,128)(2,1)}, f32[2,768]{1,0:T(2,128)}) custom-call(s32[3]{0:T(128)} %pad_add_fusion.info, bf16[8,128,768]{2,1,0:T(8,128)(2,1)} %lat_ref.5, f32[512,768]{1,0:T(8,128)} %get-tuple-element.66.grad_ref, bf16[512,768]{1,0:T(8,128)(2,1)} %get-tuple-element.75.own_ref, bf16[512,768]{1,0:T(8,128)(2,1)} %copy-done.7, ...), custom_call_target="tpu_custom_call" | custom-call | flops 7864320 | bytes 6291456 | tf_op jit(solution)/shard_map/latent_back/pallas_call | solution.py:559
  220.3 11.3 %collective-permute-done.20 = bf16[1,4,96,768]{3,2,1,0:T(8,128)(2,1)S(1)} collective-permute-done((bf16[1,4,96,768]{3,2,1,0:T(8,128)(2,1)S(1)}, bf16[1,4,96,768]{3,2,1,0:T(8,128)(2,1)S(1)}, u32[]{:S(2)}, u32[]{:S(2)}) %collective-permute-start.20) | collective-permute-done | bytes 589856 | tf_op jit(solution)/shard_map/ppermute | solution.py:52
  231.9 4.6 %collective-permute-start.21 = (bf16[1,2,96,768]{3,2,1,0:T(8,128)(2,1)S(1)}, bf16[1,2,96,768]{3,2,1,0:T(8,128)(2,1)S(1)}, u32[]{:S(2)}, u32[]{:S(2)}) collective-permute-start(bf16[1,2,96,768]{3,2,1,0:T(8,128)(2,1)S(1)} %fusion.15), channel_id=1, source_target_pairs={{0,8},{4,12},{8,0},{12,4},{16,24},{20,28},{24,16},{28,20},{1,9},{5... | collective-permute-start | bytes 884744 | tf_op jit(solution)/shard_map/ppermute | solution.py:52
  236.7 6.3 %collective-permute-done.21 = bf16[1,2,96,768]{3,2,1,0:T(8,128)(2,1)S(1)} collective-permute-done((bf16[1,2,96,768]{3,2,1,0:T(8,128)(2,1)S(1)}, bf16[1,2,96,768]{3,2,1,0:T(8,128)(2,1)S(1)}, u32[]{:S(2)}, u32[]{:S(2)}) %collective-permute-start.21) | collective-permute-done | bytes 294944 | tf_op jit(solution)/shard_map/ppermute | solution.py:52
  243.1 13.4 %collective-permute-done.16 = bf16[2,4,96,768]{3,2,1,0:T(8,128)(2,1)S(1)} collective-permute-done((bf16[2,4,96,768]{3,2,1,0:T(8,128)(2,1)S(1)}, bf16[2,4,96,768]{3,2,1,0:T(8,128)(2,1)S(1)}, u32[]{:S(2)}, u32[]{:S(2)}) %collective-permute-start.16) | collective-permute-done | bytes 1179680 | tf_op jit(solution)/shard_map/ppermute | solution.py:52
  258.0 4.6 %collective-permute-start.17 = (bf16[2,2,96,768]{3,2,1,0:T(8,128)(2,1)}, bf16[2,2,96,768]{3,2,1,0:T(8,128)(2,1)S(1)}, u32[]{:S(2)}, u32[]{:S(2)}) collective-permute-start(bf16[2,2,96,768]{3,2,1,0:T(8,128)(2,1)} %fusion.4), channel_id=1, source_target_pairs={{0,8},{4,12},{8,0},{12,4},{16,24},{20,28},{24,16},{28,20},{1,9},{5... | collective-permute-start | bytes 1769480 | tf_op jit(solution)/shard_map/ppermute | solution.py:52
  265.6 8.1 %byte_back.1 = (bf16[4,160,768]{2,1,0:T(8,128)(2,1)}, bf16[4,160,768]{2,1,0:T(8,128)(2,1)}, f32[2,768]{1,0:T(2,128)}) custom-call(s32[3]{0:T(128)} %pad_add_fusion.info, bf16[4,640,768]{2,1,0:T(8,128)(2,1)} %get-tuple-element.77.dkv_ref, bf16[4,320,768]{2,1,0:T(8,128)(2,1)} %copy-done.2, bf16[4,640,768]{2,1,0:T(8,128)(2,1)} %get-tuple-element.78.raw_ref, ...), custom_call_target="tpu_custom_call" | custom-call | flops 1509949440 | bytes 8388608 | tf_op jit(solution)/shard_map/byte_back/pallas_call | solution.py:644
  273.8 4.6 %collective-permute-done.22 = bf16[1,1,96,768]{3,2,1,0:T(8,128)(2,1)S(1)} collective-permute-done((bf16[1,1,96,768]{3,2,1,0:T(8,128)(2,1)S(1)}, bf16[1,1,96,768]{3,2,1,0:T(8,128)(2,1)S(1)}, u32[]{:S(2)}, u32[]{:S(2)}) %collective-permute-start.22) | collective-permute-done | bytes 147488 | tf_op jit(solution)/shard_map/ppermute | solution.py:52
  284.1 11.0 %collective-permute-done.18 = bf16[2,1,96,768]{3,2,0,1:T(8,128)(2,1)S(1)} collective-permute-done((bf16[2,1,96,768]{3,2,0,1:T(8,128)(2,1)S(1)}, bf16[2,1,96,768]{3,2,0,1:T(8,128)(2,1)S(1)}, u32[]{:S(2)}, u32[]{:S(2)}) %collective-permute-start.18) | collective-permute-done | bytes 294944 | tf_op jit(solution)/shard_map/ppermute | solution.py:52
  298.0 4.3 %collective-permute-done.23 = f32[9,768]{1,0:T(8,128)S(1)} collective-permute-done((f32[9,768]{1,0:T(8,128)S(1)}, f32[9,768]{1,0:T(8,128)S(1)}, u32[]{:S(2)}, u32[]{:S(2)}) %collective-permute-start.23) | collective-permute-done | bytes 27680 | tf_op jit(solution)/shard_map/ppermute | solution.py:52
  (213 shorter events, 71.2 us)
Async XLA Ops:
  7.2 66.8 %all-gather.2.cloned.1.call-start = ((), (), s32[]{:S(2)}) async-start(), calls=%async_computation | async-start | bytes 2654208 | tf_op jit(solution)/shard_map/all_gather | solution.py:704
  10.4 11.1 %collective-permute-start = (bf16[1,96,768]{2,1,0:T(8,128)(2,1)S(1)}, bf16[1,96,768]{2,1,0:T(8,128)(2,1)S(1)}, u32[]{:S(2)}, u32[]{:S(2)}) collective-permute-start(bf16[1,96,768]{2,1,0:T(8,128)(2,1)S(1)} %bitcast.217), channel_id=1, source_target_pairs={{0,16},{4,20},{8,24},{12,28},{16,0},{20,4},{24,8},{28,12},{1,17},{... | collective-permute-start | bytes 442376 | tf_op jit(solution)/shard_map/ppermute | solution.py:52
  21.6 15.4 %collective-permute-start.1 = (bf16[2,96,768]{2,1,0:T(8,128)(2,1)S(1)}, bf16[2,96,768]{2,1,0:T(8,128)(2,1)S(1)}, u32[]{:S(2)}, u32[]{:S(2)}) collective-permute-start(bf16[2,96,768]{2,1,0:T(8,128)(2,1)S(1)} %maximum_bitcast_fusion), channel_id=1, source_target_pairs={{0,8},{4,12},{8,0},{12,4},{16,24},{20,28},{24,16},{28,20},{1,9},{5... | collective-permute-start | bytes 884744 | tf_op jit(solution)/shard_map/ppermute | solution.py:52
  37.0 17.8 %collective-permute-start.2 = (bf16[4,96,768]{2,1,0:T(8,128)(2,1)S(1)}, bf16[4,96,768]{2,1,0:T(8,128)(2,1)S(1)}, u32[]{:S(2)}, u32[]{:S(2)}) collective-permute-start(bf16[4,96,768]{2,1,0:T(8,128)(2,1)S(1)} %bitcast.216), channel_id=1, source_target_pairs={{0,4},{4,0},{8,12},{12,8},{16,20},{20,16},{24,28},{28,24},{1,5},{5... | collective-permute-start | bytes 1769480 | tf_op jit(solution)/shard_map/ppermute | solution.py:52
  55.2 29.0 %collective-permute-start.3 = (bf16[768,768]{1,0:T(8,128)(2,1)S(1)}, bf16[768,768]{1,0:T(8,128)(2,1)S(1)}, u32[]{:S(2)}, u32[]{:S(2)}) collective-permute-start(bf16[768,768]{1,0:T(8,128)(2,1)S(1)} %bitcast.210), channel_id=1, source_target_pairs={{0,1},{1,0},{2,3},{3,2},{4,5},{5,4},{6,7},{7,6},{8,9},{9,8},{10,11... | collective-permute-start | bytes 3538952 | tf_op jit(solution)/shard_map/ppermute | solution.py:52
  74.0 48.7 %collective-permute-start.6 = (bf16[768,1536]{1,0:T(8,128)(2,1)}, bf16[768,1536]{1,0:T(8,128)(2,1)}, u32[]{:S(2)}, u32[]{:S(2)}) collective-permute-start(bf16[768,1536]{1,0:T(8,128)(2,1)} %all-gather.2.cloned.1.call-done.w_own_ref.w2_own_ref), channel_id=1, source_target_pairs={{0,1},{1,0},{2,3},{3,2},{4,5},{5,4},{6,7},{7,6},{8,9},{9,8},{10,11... | collective-permute-start | bytes 7077896 | tf_op jit(solution)/shard_map/ppermute | solution.py:52
  102.5 20.2 %collective-permute-start.4 = (bf16[4,128,768]{2,1,0:T(8,128)(2,1)}, bf16[4,128,768]{2,1,0:T(8,128)(2,1)S(1)}, u32[]{:S(2)}, u32[]{:S(2)}) collective-permute-start(bf16[4,128,768]{2,1,0:T(8,128)(2,1)} %get-tuple-element.58.own_ref), channel_id=1, source_target_pairs={{0,2},{1,3},{2,0},{3,1},{4,6},{5,7},{6,4},{7,5},{8,10},{9,11},{10,... | collective-permute-start | bytes 2359304 | tf_op jit(solution)/shard_map/ppermute | solution.py:52
  135.1 20.7 %collective-permute-start.9 = (bf16[512,768]{1,0:T(8,128)(2,1)}, bf16[512,768]{1,0:T(8,128)(2,1)S(1)}, u32[]{:S(2)}, u32[]{:S(2)}) collective-permute-start(bf16[512,768]{1,0:T(8,128)(2,1)} %get-tuple-element.65.own_ref), channel_id=1, source_target_pairs={{0,2},{1,3},{2,0},{3,1},{4,6},{5,7},{6,4},{7,5},{8,10},{9,11},{10,... | collective-permute-start | bytes 2359304 | tf_op jit(solution)/shard_map/ppermute | solution.py:52
  147.7 40.2 %collective-permute-start.7 = (bf16[512,768]{1,0:T(8,128)(2,1)}, bf16[512,768]{1,0:T(8,128)(2,1)}, u32[]{:S(2)}, u32[]{:S(2)}) collective-permute-start(bf16[512,768]{1,0:T(8,128)(2,1)} %get-tuple-element.64), channel_id=1, source_target_pairs={{0,2},{1,3},{2,0},{3,1},{4,6},{5,7},{6,4},{7,5},{8,10},{9,11},{10,... | collective-permute-start | bytes 2359304 | tf_op jit(solution)/shard_map/ppermute | solution.py:52
  148.9 68.2 %collective-permute-start.15 = (bf16[2,768,768]{2,1,0:T(8,128)(2,1)}, bf16[2,768,768]{2,1,0:T(8,128)(2,1)S(1)}, u32[]{:S(2)}, u32[]{:S(2)}) collective-permute-start(bf16[2,768,768]{2,1,0:T(8,128)(2,1)} %get-tuple-element.87), channel_id=1, source_target_pairs={{0,1},{1,0},{2,3},{3,2},{4,5},{5,4},{6,7},{7,6},{8,9},{9,8},{10,11... | collective-permute-start | bytes 7077896 | tf_op jit(solution)/shard_map/ppermute | solution.py:52
  186.1 27.3 %collective-permute-start.19 = (bf16[768,768]{1,0:T(8,128)(2,1)}, bf16[768,768]{1,0:T(8,128)(2,1)S(1)}, u32[]{:S(2)}, u32[]{:S(2)}) collective-permute-start(bf16[768,768]{1,0:T(8,128)(2,1)} %get-tuple-element.89), channel_id=1, source_target_pairs={{0,1},{1,0},{2,3},{3,2},{4,5},{5,4},{6,7},{7,6},{8,9},{9,8},{10,11... | collective-permute-start | bytes 3538952 | tf_op jit(solution)/shard_map/ppermute | solution.py:52
  186.2 20.6 %collective-permute-start.10 = (bf16[512,768]{1,0:T(8,128)(2,1)}, bf16[512,768]{1,0:T(8,128)(2,1)S(1)}, u32[]{:S(2)}, u32[]{:S(2)}) collective-permute-start(bf16[512,768]{1,0:T(8,128)(2,1)} %get-tuple-element.75.own_ref), channel_id=1, source_target_pairs={{0,2},{1,3},{2,0},{3,1},{4,6},{5,7},{6,4},{7,5},{8,10},{9,11},{10,... | collective-permute-start | bytes 2359304 | tf_op jit(solution)/shard_map/ppermute | solution.py:52
  189.3 24.0 %collective-permute-start.8 = (bf16[4,128,768]{2,1,0:T(8,128)(2,1)S(1)}, bf16[4,128,768]{2,1,0:T(8,128)(2,1)S(1)}, u32[]{:S(2)}, u32[]{:S(2)}) collective-permute-start(bf16[4,128,768]{2,1,0:T(8,128)(2,1)S(1)} %bitcast.214), channel_id=1, source_target_pairs={{0,1},{1,0},{2,3},{3,2},{4,5},{5,4},{6,7},{7,6},{8,9},{9,8},{10,11... | collective-permute-start | bytes 2359304 | tf_op jit(solution)/shard_map/ppermute | solution.py:52
  197.7 66.6 %collective-permute-start.12 = (bf16[4,320,768]{2,1,0:T(8,128)(2,1)}, bf16[4,320,768]{2,1,0:T(8,128)(2,1)S(1)}, u32[]{:S(2)}, u32[]{:S(2)}) collective-permute-start(bf16[4,320,768]{2,1,0:T(8,128)(2,1)} %byte_send.1), channel_id=1, source_target_pairs={{0,2},{1,3},{2,0},{3,1},{4,6},{5,7},{6,4},{7,5},{8,10},{9,11},{10,... | collective-permute-start | bytes 5898248 | tf_op jit(solution)/shard_map/ppermute | solution.py:52
  212.6 23.9 %collective-permute-start.11 = (bf16[4,128,768]{2,1,0:T(8,128)(2,1)}, bf16[4,128,768]{2,1,0:T(8,128)(2,1)S(1)}, u32[]{:S(2)}, u32[]{:S(2)}) collective-permute-start(bf16[4,128,768]{2,1,0:T(8,128)(2,1)} %get-tuple-element.76), channel_id=1, source_target_pairs={{0,1},{1,0},{2,3},{3,2},{4,5},{5,4},{6,7},{7,6},{8,9},{9,8},{10,11... | collective-permute-start | bytes 2359304 | tf_op jit(solution)/shard_map/ppermute | solution.py:52
  215.4 16.2 %collective-permute-start.20 = (bf16[1,4,96,768]{3,2,1,0:T(8,128)(2,1)S(1)}, bf16[1,4,96,768]{3,2,1,0:T(8,128)(2,1)S(1)}, u32[]{:S(2)}, u32[]{:S(2)}) collective-permute-start(bf16[1,4,96,768]{3,2,1,0:T(8,128)(2,1)S(1)} %fusion.5), channel_id=1, source_target_pairs={{0,4},{4,0},{8,12},{12,8},{16,20},{20,16},{24,28},{28,24},{1,5},{5... | collective-permute-start | bytes 1769480 | tf_op jit(solution)/shard_map/ppermute | solution.py:52
  218.0 38.5 %collective-permute-start.16 = (bf16[2,4,96,768]{3,2,1,0:T(8,128)(2,1)S(1)}, bf16[2,4,96,768]{3,2,1,0:T(8,128)(2,1)S(1)}, u32[]{:S(2)}, u32[]{:S(2)}) collective-permute-start(bf16[2,4,96,768]{3,2,1,0:T(8,128)(2,1)S(1)} %fusion), channel_id=1, source_target_pairs={{0,4},{4,0},{8,12},{12,8},{16,20},{20,16},{24,28},{28,24},{1,5},{5... | collective-permute-start | bytes 3538952 | tf_op jit(solution)/shard_map/ppermute | solution.py:52
  231.9 11.2 %collective-permute-start.21 = (bf16[1,2,96,768]{3,2,1,0:T(8,128)(2,1)S(1)}, bf16[1,2,96,768]{3,2,1,0:T(8,128)(2,1)S(1)}, u32[]{:S(2)}, u32[]{:S(2)}) collective-permute-start(bf16[1,2,96,768]{3,2,1,0:T(8,128)(2,1)S(1)} %fusion.15), channel_id=1, source_target_pairs={{0,8},{4,12},{8,0},{12,4},{16,24},{20,28},{24,16},{28,20},{1,9},{5... | collective-permute-start | bytes 884744 | tf_op jit(solution)/shard_map/ppermute | solution.py:52
  258.0 21.2 %collective-permute-start.17 = (bf16[2,2,96,768]{3,2,1,0:T(8,128)(2,1)}, bf16[2,2,96,768]{3,2,1,0:T(8,128)(2,1)S(1)}, u32[]{:S(2)}, u32[]{:S(2)}) collective-permute-start(bf16[2,2,96,768]{3,2,1,0:T(8,128)(2,1)} %fusion.4), channel_id=1, source_target_pairs={{0,8},{4,12},{8,0},{12,4},{16,24},{20,28},{24,16},{28,20},{1,9},{5... | collective-permute-start | bytes 1769480 | tf_op jit(solution)/shard_map/ppermute | solution.py:52
  262.6 15.8 %collective-permute-start.22 = (bf16[1,1,96,768]{3,2,1,0:T(8,128)(2,1)S(1)}, bf16[1,1,96,768]{3,2,1,0:T(8,128)(2,1)S(1)}, u32[]{:S(2)}, u32[]{:S(2)}) collective-permute-start(bf16[1,1,96,768]{3,2,1,0:T(8,128)(2,1)S(1)} %fusion.19), channel_id=1, source_target_pairs={{0,16},{4,20},{8,24},{12,28},{16,0},{20,4},{24,8},{28,12},{1,17},{... | collective-permute-start | bytes 442376 | tf_op jit(solution)/shard_map/ppermute | solution.py:52
  273.7 38.3 %collective-permute-start.13 = (bf16[4,160,768]{2,1,0:T(8,128)(2,1)}, bf16[4,160,768]{2,1,0:T(8,128)(2,1)S(1)}, u32[]{:S(2)}, u32[]{:S(2)}) collective-permute-start(bf16[4,160,768]{2,1,0:T(8,128)(2,1)} %get-tuple-element.80), channel_id=1, source_target_pairs={{0,1},{1,0},{2,3},{3,2},{4,5},{5,4},{6,7},{7,6},{8,9},{9,8},{10,11... | collective-permute-start | bytes 2949128 | tf_op jit(solution)/shard_map/ppermute | solution.py:52
  279.4 15.7 %collective-permute-start.18 = (bf16[2,1,96,768]{3,2,0,1:T(8,128)(2,1)S(1)}, bf16[2,1,96,768]{3,2,0,1:T(8,128)(2,1)S(1)}, u32[]{:S(2)}, u32[]{:S(2)}) collective-permute-start(bf16[2,1,96,768]{3,2,0,1:T(8,128)(2,1)S(1)} %fusion.14), channel_id=1, source_target_pairs={{0,16},{4,20},{8,24},{12,28},{16,0},{20,4},{24,8},{28,12},{1,17},{... | collective-permute-start | bytes 884744 | tf_op jit(solution)/shard_map/ppermute | solution.py:52
  297.2 5.1 %collective-permute-start.23 = (f32[9,768]{1,0:T(8,128)S(1)}, f32[9,768]{1,0:T(8,128)S(1)}, u32[]{:S(2)}, u32[]{:S(2)}) collective-permute-start(f32[9,768]{1,0:T(8,128)S(1)} %concatenate.47), channel_id=1, source_target_pairs={{0,16},{4,20},{8,24},{12,28},{16,0},{20,4},{24,8},{28,12},{1,17},{... | collective-permute-start | bytes 82952 | tf_op jit(solution)/shard_map/ppermute | solution.py:52
  306.5 4.2 %collective-permute-start.25 = (f32[9,768]{1,0:T(8,128)S(1)}, f32[9,768]{1,0:T(8,128)S(1)}, u32[]{:S(2)}, u32[]{:S(2)}) collective-permute-start(f32[9,768]{1,0:T(8,128)S(1)} %add.176), channel_id=1, source_target_pairs={{0,4},{4,0},{8,12},{12,8},{16,20},{20,16},{24,28},{28,24},{1,5},{5... | collective-permute-start | bytes 82952 | tf_op jit(solution)/shard_map/ppermute | solution.py:52
  (45 other events, 326.2 us)
Sparse Core Ops, SparseCore 0:
  10.8 63.1 all-gather.1
